TPU v7x, 512 devices: a whole 4x8x8 slice. The times are simulated.
512 devices in a mesh: row: 32 (over z_hi, x, core), col: 16 (over z_lo, y).
Axes of the slice: x: 4, y: 8, z: 8 (z_hi: 4, z_lo: 2; z = z_hi * 2 + z_lo), core: 2. Of those that a mesh axis runs over, the one named last changes fastest.
Arguments:
- pair: float32 [768, 768, 128], P('row', 'col'), may hold values from -120 to 120
- residue_mask: int32 [768], replicated, may hold values from 0 to 1, as said below
- start_proj: bfloat16 [128, 512], replicated, may hold values from -0.5 to 0.5
- start_bias_w: bfloat16 [128, 4], replicated, may hold values from -16 to 16
- start_out: bfloat16 [128, 128], replicated, may hold values from -1 to 1
- end_proj: bfloat16 [128, 512], replicated, may hold values from -0.5 to 0.5
- end_bias_w: bfloat16 [128, 4], replicated, may hold values from -16 to 16
- end_out: bfloat16 [128, 128], replicated, may hold values from -1 to 1
Outputs:
- pair_out: float32 [768, 768, 128], P('row', 'col')
Inputs may be any that keep to these rules, and one draw needn't show every extreme that they name: `residue_mask`: the first residue is always present.
All inputs are finite; a program needn't handle non-finite values.
Results may differ from a plain program's by a relative error of at most 0.023.
The roundings to bfloat16 on the way count: a program that leaves them out, or rounds other values in their place, can miss the bound.
Values may be sent and summed in bfloat16 or wider, within the bound.
A program may use at most 64 MiB of HBM per device.

v0:
```python
import jax
import jax.numpy as jnp
from jax import lax
from jax.sharding import PartitionSpec as P

C = 128
HEADS = 4
HD = 32


def normalize(field):
    mean = jnp.mean(field, axis=-1, keepdims=True)
    centered = field - mean
    var = jnp.mean(centered * centered, axis=-1, keepdims=True)
    return (centered * lax.rsqrt(var + 1e-05)).astype(jnp.bfloat16)


def project(normed, proj_w):
    lead = normed.shape[:2]
    mixed = jnp.dot(normed.reshape(-1, C), proj_w, preferred_element_type=jnp.float32)
    mixed = mixed.reshape(lead + (4, HEADS, HD))
    query = mixed[:, :, 0] * HD ** (-0.5)
    gate = jax.nn.sigmoid(mixed[:, :, 3])
    return jnp.stack([query, mixed[:, :, 1], mixed[:, :, 2], gate], axis=2).astype(jnp.bfloat16)


def head_bias(normed, bias_w):
    lead = normed.shape[:2]
    flat = jnp.dot(normed.reshape(-1, C), bias_w, preferred_element_type=jnp.float32)
    return flat.astype(jnp.bfloat16).reshape(lead + (HEADS,))


def attend(lanes, piece, residue_mask):
    bias = piece[0].astype(jnp.float32)
    keep = residue_mask > 0

    def one_item(item):
        selected, whole = item
        scores = (
            jnp.einsum(
                "qd,kd->qk",
                selected[:, :HD],
                whole[:, HD : 2 * HD],
                preferred_element_type=jnp.float32,
            )
            + bias
        )
        scores = jnp.where(keep[None, :], scores, -1000000000.0)
        weights = jax.nn.softmax(scores, axis=-1).astype(jnp.bfloat16)
        out = jnp.dot(weights, whole[:, 2 * HD : 3 * HD], preferred_element_type=jnp.float32)
        return (out * selected[:, 3 * HD :]).astype(jnp.bfloat16)

    return lax.map(one_item, (lanes, lanes))


def shards(pair, residue_mask, start_proj, start_bias_w, start_out, end_proj, end_bias_w, end_out):
    rows, cols = (pair.shape[0], pair.shape[1])
    n_row = lax.axis_size("row")
    n_col = lax.axis_size("col")
    group = n_col // HEADS
    quarter = n_row // HEADS
    normed = normalize(pair)
    packed = project(normed, start_proj)
    items = rows // group
    send = packed.reshape(group, items, cols, 4, HEADS, HD).transpose(4, 0, 1, 2, 3, 5)
    send = send.reshape(n_col, items, cols, 4 * HD)
    bias = head_bias(normed, start_bias_w).transpose(2, 0, 1)
    tall = lax.all_gather(bias, "row", axis=1, tiled=True)
    bias_send = jnp.repeat(tall, group, axis=0)
    moved, bias_moved = (
        lax.all_to_all(send, "col", split_axis=0, concat_axis=2, tiled=True),
        lax.all_to_all(bias_send, "col", split_axis=0, concat_axis=2, tiled=True),
    )
    lanes = moved[0]
    attended = attend(lanes, bias_moved, residue_mask)
    back = lax.all_to_all(attended, "col", split_axis=1, concat_axis=0, tiled=True)
    merged = (
        back.reshape(HEADS, group, items, cols, HD).transpose(1, 2, 3, 0, 4).reshape(rows * cols, C)
    )
    pair_mid = pair + jnp.dot(merged, start_out, preferred_element_type=jnp.float32).reshape(
        rows, cols, C
    )
    normed2 = normalize(pair_mid)
    packed2 = project(normed2, end_proj)
    width = cols // quarter
    send2 = packed2.reshape(rows, quarter, width, 4, HEADS, HD).transpose(4, 1, 2, 0, 3, 5)
    send2 = send2.reshape(n_row, width, rows, 4 * HD)
    bias2 = head_bias(normed2, end_bias_w).transpose(2, 1, 0)
    broad = lax.all_gather(bias2, "col", axis=1, tiled=True)
    bias_send2 = jnp.repeat(broad, quarter, axis=0)
    moved2, bias_moved2 = (
        lax.all_to_all(send2, "row", split_axis=0, concat_axis=2, tiled=True),
        lax.all_to_all(bias_send2, "row", split_axis=0, concat_axis=2, tiled=True),
    )
    lanes2 = moved2[0]
    attended2 = attend(lanes2, bias_moved2, residue_mask)
    back2 = lax.all_to_all(attended2, "row", split_axis=1, concat_axis=0, tiled=True)
    merged2 = (
        back2.reshape(HEADS, quarter, width, rows, HD)
        .transpose(3, 1, 2, 0, 4)
        .reshape(rows * cols, C)
    )
    return pair_mid + jnp.dot(merged2, end_out, preferred_element_type=jnp.float32).reshape(
        rows, cols, C
    )


def solution(mesh):
    placed = (P("row", "col", None), P(), P(), P(), P(), P(), P(), P())
    return jax.shard_map(
        shards, mesh=mesh, in_specs=placed, out_specs=P("row", "col", None), check_vma=False
    )
```

profile of v0, /device:TPU:1, one launch (start us, length us, event | category | flops | bytes accessed | tf_op | source)
XLA Modules:
  0.0 317.9 jit_solution(10700369373773776018)
XLA Ops:
  0.0 1.0 copy.57
  1.0 1.3 reduce_sum.54
  2.3 1.5 multiply_reduce_fusion.1
  3.8 1.4 multiply_convert_fusion.1
  5.3 1.0 fusion.30
  7.2 1.0 pad_maximum_fusion
  8.2 2.4 copy.61
  10.5 9.6 %all-to-all-start = ((bf16[16,6,48,128]{3,2,1,0:T(8,128)(2,1)}), bf16[16,6,48,128]{3,2,1,0:T(8,128)(2,1)S(1)}, u32[]{:S(2)}, u32[]{:S(2)}) async-start(bf16[16,6,48,128]{3,2,1,0:T(8,128)(2,1)} %copy.61), calls=%async_computation | async-start | bytes 2359296 | tf_op jit(solution)/shard_map/all_to_all | solution.py:71
  20.4 52.8 %all_gather.6 = bf16[4,768,48]{2,1,0:T(8,128)(2,1)S(1)} all-gather(bf16[4,24,48]{2,1,0:T(8,128)(2,1)S(1)} %bitcast.147), channel_id=1, replica_groups=mesh['row'=32,'col'=16] {'row'}, dimensions={1}, use_global_device_ids=true | all-gather | bytes 304128 | tf_op jit(solution)/shard_map/all_gather | solution.py:68
  73.5 1.1 broadcast_in_dim.43
  74.6 8.5 %all-to-all-start.1 = ((bf16[16,768,48]{1,2,0:T(8,128)(2,1)}), bf16[16,768,48]{1,2,0:T(8,128)(2,1)}, u32[]{:S(2)}, u32[]{:S(2)}) async-start(bf16[16,768,48]{1,2,0:T(8,128)(2,1)} %bitcast.19), calls=%async_computation.1 | async-start | bytes 2359296 | tf_op jit(solution)/shard_map/all_to_all | solution.py:72
  83.1 1.1 copy.62
  84.2 26.7 %all-to-all-done.1 = bf16[16,768,48]{1,2,0:T(8,128)(2,1)} async-done(((bf16[16,768,48]{1,2,0:T(8,128)(2,1)}), bf16[16,768,48]{1,2,0:T(8,128)(2,1)}, u32[]{:S(2)}, u32[]{:S(2)}) %all-to-all-start.1) | async-done | bytes 1179680 | tf_op jit(solution)/shard_map/all_to_all | solution.py:72
  110.9 1.5 bitcast_convert_fusion.1
  112.5 15.1 %while.20 = (s32[]{:T(128)}, bf16[6,768,32]{1,2,0:T(8,128)(2,1)S(1)}, pred[768]{0:T(1024)(128)(4,1)S(1)}, bf16[6,768,128]{2,1,0:T(8,128)(2,1)}, f32[768,768]{0,1:T(8,128)S(1)}, /*index=5*/s32[]{:T(128)}) while((s32[]{:T(128)}, bf16[6,768,32]{1,2,0:T(8,128)(2,1)S(1)}, pred[768]{0:T(1024)(128)(4,1)S(1)}, bf16[6,768,128]{2,1,0:T(8,128)(2,1)}, ...), condition=%wide.region_5.6_spmd, body=%wide.region_2.5_spmd.sunk | while | flops 80288256 | bytes 10487893 | solution.py:53
  112.5 0.9 constant_dynamic-slice_fusion.4
  115.0 0.9 constant_dynamic-slice_fusion.4
  117.5 0.9 constant_dynamic-slice_fusion.4
  120.1 0.9 constant_dynamic-slice_fusion.4
  122.6 0.9 constant_dynamic-slice_fusion.4
  125.1 0.9 constant_dynamic-slice_fusion.4
  127.6 1.1 copy.65
  128.7 1.9 reshape.126
  130.6 6.7 %all-to-all-start.2 = ((bf16[16,2,4608]{2,1,0:T(2,128)(2,1)}), bf16[16,2,4608]{2,1,0:T(2,128)(2,1)S(1)}, u32[]{:S(2)}, u32[]{:S(2)}) async-start(bf16[16,2,4608]{2,1,0:T(2,128)(2,1)} %reshape.126), calls=%async_computation.2 | async-start | bytes 589824 | tf_op jit(solution)/shard_map/all_to_all | solution.py:76
  137.4 9.2 %all-to-all-done.2 = bf16[16,2,4608]{2,1,0:T(2,128)(2,1)S(1)} async-done(((bf16[16,2,4608]{2,1,0:T(2,128)(2,1)}), bf16[16,2,4608]{2,1,0:T(2,128)(2,1)S(1)}, u32[]{:S(2)}, u32[]{:S(2)}) %all-to-all-start.2) | async-done | bytes 294944 | tf_op jit(solution)/shard_map/all_to_all | solution.py:76
  146.6 1.0 reshape.127
  147.7 1.6 copy.68
  149.3 1.6 fusion.36
  151.7 1.0 fusion.28
  152.7 1.3 fusion.21
  154.0 1.6 slice.108
  155.5 1.8 copy.73
  157.4 4.8 %copy.72 = bf16[24,48,2,4,32]{4,0,3,2,1:T(8,128)(2,1)S(1)} copy(bf16[24,48,2,4,32]{1,4,3,2,0:T(8,128)(2,1)} %slice.108) | data formatting | bytes 1179648 | tf_op jit(solution)/shard_map/slice | solution.py:24
  162.2 2.8 copy.71
  165.0 2.3 maximum_bitcast_fusion
  167.3 5.8 %copy.76 = bf16[4,8,6,24,4,32]{5,4,3,2,1,0:T(4,128)(2,1)} copy(bf16[4,8,6,24,4,32]{5,3,0,4,2,1:T(8,128)(2,1)S(1)} %maximum_bitcast_fusion) | data formatting | bytes 2359296 | tf_op jit(solution)/shard_map/transpose | solution.py:86
  173.1 6.4 %reshape.111 = bf16[32,6,24,128]{3,2,1,0:T(8,128)(2,1)} reshape(bf16[4,8,6,24,4,32]{5,4,3,2,1,0:T(4,128)(2,1)} %copy.76) | data formatting | bytes 2359296 | tf_op jit(solution)/shard_map/reshape | solution.py:87
  179.5 8.6 %all-to-all-start.3 = ((bf16[32,6,24,128]{3,2,1,0:T(8,128)(2,1)}), bf16[32,6,24,128]{3,2,1,0:T(8,128)(2,1)S(1)}, u32[]{:S(2)}, u32[]{:S(2)}) async-start(bf16[32,6,24,128]{3,2,1,0:T(8,128)(2,1)} %reshape.111), calls=%async_computation.3 | async-start | bytes 2359296 | tf_op jit(solution)/shard_map/all_to_all | solution.py:92
  188.6 32.2 %all_gather.7 = bf16[4,768,24]{2,0,1:T(4,128)(2,1)S(1)} all-gather(bf16[4,48,24]{2,0,1:T(4,128)(2,1)S(1)} %bitcast.146), channel_id=1, replica_groups=mesh['row'=32,'col'=16] {'col'}, dimensions={1}, use_global_device_ids=true | all-gather | bytes 156672 | tf_op jit(solution)/shard_map/all_gather | solution.py:89
  221.3 5.4 %all-to-all-done.3 = bf16[32,6,24,128]{3,2,1,0:T(8,128)(2,1)S(1)} async-done(((bf16[32,6,24,128]{3,2,1,0:T(8,128)(2,1)}), bf16[32,6,24,128]{3,2,1,0:T(8,128)(2,1)S(1)}, u32[]{:S(2)}, u32[]{:S(2)}) %all-to-all-start.3) | async-done | bytes 1179680 | tf_op jit(solution)/shard_map/all_to_all | solution.py:92
  226.6 1.1 broadcast_in_dim.44
  227.7 11.2 %all-to-all-start.4 = ((bf16[32,768,24]{1,2,0:T(8,128)(2,1)}), bf16[32,768,24]{1,2,0:T(8,128)(2,1)}, u32[]{:S(2)}, u32[]{:S(2)}) async-start(bf16[32,768,24]{1,2,0:T(8,128)(2,1)} %bitcast.47), calls=%async_computation.4 | async-start | bytes 2359296 | tf_op jit(solution)/shard_map/all_to_all | solution.py:93
  239.0 1.2 copy.77
  240.2 26.7 %all-to-all-done.4 = bf16[32,768,24]{1,2,0:T(8,128)(2,1)} async-done(((bf16[32,768,24]{1,2,0:T(8,128)(2,1)}), bf16[32,768,24]{1,2,0:T(8,128)(2,1)}, u32[]{:S(2)}, u32[]{:S(2)}) %all-to-all-start.4) | async-done | bytes 1179680 | tf_op jit(solution)/shard_map/all_to_all | solution.py:93
  266.9 1.4 bitcast_convert_fusion
  269.0 18.8 %while.21 = (s32[]{:T(128)}, bf16[6,768,32]{1,2,0:T(8,128)(2,1)}, pred[768]{0:T(1024)(128)(4,1)S(1)}, bf16[6,768,128]{2,1,0:T(8,128)(2,1)}, f32[768,768]{0,1:T(8,128)S(1)}, /*index=5*/s32[]{:T(128)}) while((s32[]{:T(128)}, bf16[6,768,32]{1,2,0:T(8,128)(2,1)}, pred[768]{0:T(1024)(128)(4,1)S(1)}, bf16[6,768,128]{2,1,0:T(8,128)(2,1)}, ...), condition=%wide.region_11.12_spmd, body=%wide.region_8.11_spmd.sunk | while | flops 80288256 | bytes 10487893 | solution.py:53
  269.0 0.9 constant_dynamic-slice_fusion.5
  271.0 1.1 fusion.63
  272.2 0.9 constant_dynamic-slice_fusion.5
  274.2 1.1 fusion.63
  275.3 0.9 constant_dynamic-slice_fusion.5
  277.3 1.1 fusion.63
  278.5 0.9 constant_dynamic-slice_fusion.5
  280.5 1.1 fusion.63
  281.6 0.9 constant_dynamic-slice_fusion.5
  283.6 1.1 fusion.63
  284.7 0.9 constant_dynamic-slice_fusion.5
  286.7 1.1 fusion.63
  287.9 1.9 copy.81
  289.8 1.1 reshape.128
  291.0 22.7 %all_to_all.78 = bf16[32,2,2304]{2,1,0:T(2,128)(2,1)S(1)} all-to-all(bf16[32,2,2304]{2,1,0:T(2,128)(2,1)S(1)} %reshape.128), channel_id=1, replica_groups=mesh['row'=32,'col'=16] {'row'}, dimensions={0} | all-to-all | bytes 589824 | tf_op jit(solution)/shard_map/all_to_all | solution.py:97
  313.7 1.0 reshape.129
  314.7 1.5 copy.84
  316.9 1.0 convolution_add_fusion
  (79 shorter events, 20.3 us)
Async XLA Ops:
  0.0 149.3 %copy-start = (bf16[128,128]{1,0:T(8,128)(2,1)S(1)}, bf16[128,128]{1,0:T(8,128)(2,1)}, u32[]{:S(2)}) copy-start(bf16[128,128]{1,0:T(8,128)(2,1)} %param.16) | copy-start | bytes 98308
  8.2 11.9 %copy-start.6 = (bf16[128,4]{0,1:T(4,128)(2,1)S(1)}, bf16[128,4]{0,1:T(4,128)(2,1)}, u32[]{:S(2)}) copy-start(bf16[128,4]{0,1:T(4,128)(2,1)} %param.15) | copy-start | bytes 3076
  10.5 63.0 %all-to-all-start = ((bf16[16,6,48,128]{3,2,1,0:T(8,128)(2,1)}), bf16[16,6,48,128]{3,2,1,0:T(8,128)(2,1)S(1)}, u32[]{:S(2)}, u32[]{:S(2)}) async-start(bf16[16,6,48,128]{3,2,1,0:T(8,128)(2,1)} %copy.61), calls=%async_computation | async-start | bytes 2359296 | tf_op jit(solution)/shard_map/all_to_all | solution.py:71
  73.2 9.9 %copy-start.5 = (s32[768]{0:T(1024)S(1)}, s32[768]{0:T(1024)}, u32[]{:S(2)}) copy-start(s32[768]{0:T(1024)} %param.13) | copy-start | bytes 9220
  74.6 36.3 %all-to-all-start.1 = ((bf16[16,768,48]{1,2,0:T(8,128)(2,1)}), bf16[16,768,48]{1,2,0:T(8,128)(2,1)}, u32[]{:S(2)}, u32[]{:S(2)}) async-start(bf16[16,768,48]{1,2,0:T(8,128)(2,1)} %bitcast.19), calls=%async_computation.1 | async-start | bytes 2359296 | tf_op jit(solution)/shard_map/all_to_all | solution.py:72
  127.6 9.7 %copy-start.3 = (bf16[128,512]{1,0:T(8,128)(2,1)S(1)}, bf16[128,512]{1,0:T(8,128)(2,1)}, u32[]{:S(2)}) copy-start(bf16[128,512]{1,0:T(8,128)(2,1)} %param.17) | copy-start | bytes 393220
  130.6 16.0 %all-to-all-start.2 = ((bf16[16,2,4608]{2,1,0:T(2,128)(2,1)}), bf16[16,2,4608]{2,1,0:T(2,128)(2,1)S(1)}, u32[]{:S(2)}, u32[]{:S(2)}) async-start(bf16[16,2,4608]{2,1,0:T(2,128)(2,1)} %reshape.126), calls=%async_computation.2 | async-start | bytes 589824 | tf_op jit(solution)/shard_map/all_to_all | solution.py:76
  137.3 12.0 %copy-start.2 = (f32[24,48,128]{2,1,0:T(8,128)S(1)}, f32[24,48,128]{2,1,0:T(8,128)}, u32[]{:S(2)}) copy-start(f32[24,48,128]{2,1,0:T(8,128)} %param.12) | copy-start | bytes 1769476
  179.5 8.6 %copy-start.7 = (bf16[128,4]{0,1:T(4,128)(2,1)S(1)}, bf16[128,4]{0,1:T(4,128)(2,1)}, u32[]{:S(2)}) copy-start(bf16[128,4]{0,1:T(4,128)(2,1)} %param.18) | copy-start | bytes 3076
  179.5 47.1 %all-to-all-start.3 = ((bf16[32,6,24,128]{3,2,1,0:T(8,128)(2,1)}), bf16[32,6,24,128]{3,2,1,0:T(8,128)(2,1)S(1)}, u32[]{:S(2)}, u32[]{:S(2)}) async-start(bf16[32,6,24,128]{3,2,1,0:T(8,128)(2,1)} %reshape.111), calls=%async_computation.3 | async-start | bytes 2359296 | tf_op jit(solution)/shard_map/all_to_all | solution.py:92
  227.7 39.1 %all-to-all-start.4 = ((bf16[32,768,24]{1,2,0:T(8,128)(2,1)}), bf16[32,768,24]{1,2,0:T(8,128)(2,1)}, u32[]{:S(2)}, u32[]{:S(2)}) async-start(bf16[32,768,24]{1,2,0:T(8,128)(2,1)} %bitcast.47), calls=%async_computation.4 | async-start | bytes 2359296 | tf_op jit(solution)/shard_map/all_to_all | solution.py:93
  314.7 2.1 copy-start.4
  314.7 3.2 copy-start.1
where the time goes:
time: 319 us; the launch traced here: 318 us
  blocking collectives  108 us (34%)
  waiting for transfers between devices  67.9 us (21%)
  local copies, waits for them, and re-layouts  58.3 us (18%)
  starting transfers between devices  44.6 us (14%)
  matrix products  21.3 us (7%)
  other arithmetic  17.5 us (5%)
    all_gather x1, blocking collectives, shards(): tall = lax.all_gather(bias, 'row', axis=1, tiled=True)  52.8 us
    all_gather x1, blocking collectives, shards(): broad = lax.all_gather(bias2, 'col', axis=1, tiled=True)  32.2 us
    all_to_all x1, waiting for transfers between devices, shards(): lax.all_to_all(bias_send, 'col', split_axis=0, concat_axis=2, tiled=True)  26.7 us
    all_to_all x1, waiting for transfers between devices, shards(): lax.all_to_all(bias_send2, 'row', split_axis=0, concat_axis=2, tiled=True)  26.7 us
    all_to_all x1, blocking collectives, shards(): lax.all_to_all(attended2, 'row', split_axis=1, concat_axis=0, tiled=True)  22.7 us
    dynamic_slice x24, local copies, waits for them, and re-layouts, attend(): return lax.map(one_item, (lanes, lanes))  13.1 us
    all_to_all x1, starting transfers between devices, shards(): lax.all_to_all(bias_send2, 'row', split_axis=0, concat_axis=2, tiled=True)  11.2 us
    dot_general x12, matrix products, one_item(): jnp.dot(weights, whole[:, 2 * HD:3 * HD], preferred_element_type=jnp.floa...  9.9 us
  transfers between devices with their start and end apart: 5, of which 4 were waited for; matrix products, arithmetic and copies ran while one was open for 1% of the time, Pallas kernels for 0%

commit v1 on v0

--- a/solution.py
+++ b/solution.py
@@ -1,11 +1,426 @@
+import functools
+
 import jax
 import jax.numpy as jnp
 from jax import lax
+from jax.experimental import pallas as pl
+from jax.experimental.pallas import tpu as pltpu
 from jax.sharding import PartitionSpec as P
 
 C = 128
 HEADS = 4
 HD = 32
+MESH = pl.DeviceIdType.MESH
+F32 = jnp.float32
+BF16 = jnp.bfloat16
+NT = (((1,), (1,)), ((), ()))
+NEG = -1000000000.0
+
+
+def iota(shape, dim):
+    return lax.broadcasted_iota(jnp.int32, shape, dim)
+
+
+def dot(a, b):
+    return jnp.dot(a, b, preferred_element_type=F32)
+
+
+def dot_nt(a, b):
+    return lax.dot_general(a, b, NT, preferred_element_type=F32)
+
+
+class Place:
+    def __init__(self):
+        r, c = lax.axis_index("row"), lax.axis_index("col")
+        self.zh, self.x, self.co = r // 8, (r // 2) % 4, r % 2
+        self.zl, self.y = c // 8, c % 8
+
+    def dev(self, zh=None, x=None, co=None, zl=None, y=None):
+        zh = self.zh if zh is None else zh
+        x = self.x if x is None else x
+        co = self.co if co is None else co
+        zl = self.zl if zl is None else zl
+        y = self.y if y is None else y
+        return (zh * 8 + x * 2 + co, zl * 8 + y)
+
+
+def send(src, dst, ssem, rsem, device):
+    copy = pltpu.make_async_remote_copy(
+        src_ref=src, dst_ref=dst, send_sem=ssem, recv_sem=rsem, device_id=device, device_id_type=MESH
+    )
+    copy.start()
+    return copy
+
+
+def got(dst, sem, device):
+    pltpu.make_async_remote_copy(
+        src_ref=dst, dst_ref=dst, send_sem=sem, recv_sem=sem, device_id=device, device_id_type=MESH
+    ).wait_recv()
+
+
+def sent(src, sem, device):
+    pltpu.make_async_remote_copy(
+        src_ref=src, dst_ref=src, send_sem=sem, recv_sem=sem, device_id=device, device_id_type=MESH
+    ).wait_send()
+
+
+def layer_norm(field):
+    mean = jnp.mean(field, axis=-1, keepdims=True)
+    centered = field - mean
+    var = jnp.mean(centered * centered, axis=-1, keepdims=True)
+    return centered * lax.rsqrt(var + 1e-05)
+
+
+def local_bias(normed, bias_w, spread):
+    flat = lax.dot_general(bias_w, normed, (((0,), (1,)), ((), ())), preferred_element_type=F32)
+    spread[...] = jnp.zeros_like(spread)
+    for r in range(24):
+        spread[4 * r : 4 * r + 4, 0:48] = flat[:, 48 * r : 48 * r + 48]
+    return spread[...].astype(BF16)
+
+
+def join_columns(blocks, joined):
+    total = None
+    for b in range(8):
+        lane, col = iota((128, 384), 0), iota((128, 384), 1)
+        place = jnp.where((col == lane + 48 * b) & (lane < 48), 1.0, 0.0).astype(BF16)
+        part = dot(blocks[b], place)
+        total = part if total is None else total + part
+    for j in range(3):
+        joined[j] = total[:, 128 * j : 128 * j + 128]
+
+
+def head_rows(joined, h):
+    rows = jnp.concatenate([joined[j, pl.ds(h, 24, stride=4), :] for j in range(3)], axis=1)
+    return jnp.concatenate([rows, jnp.zeros((8, 384), F32)], axis=0).astype(BF16)
+
+
+def pick(head, at):
+    row, col = iota((128, 128), 0), iota((128, 128), 1)
+    hit = (row - 32 * head == col - at) & (col >= at) & (col < at + 32)
+    return jnp.where(hit, 1.0, 0.0).astype(BF16)
+
+
+def spread_out(out_w, wide):
+    wide[...] = jnp.zeros_like(wide)
+    for h in range(HEADS):
+        for a in range(3):
+            wide[h * 128 + 32 * a : h * 128 + 32 * a + 32, a * 128 : a * 128 + 128] = out_w[
+                32 * h : 32 * h + 32, :
+            ]
+
+
+STEP = (0, 1, 3, 2)
+
+
+def scratch1():
+    dma = pltpu.SemaphoreType.DMA
+    return {
+        "nrm": pltpu.VMEM((8, 144, C), BF16),
+        "x1": pltpu.VMEM((2, 2, 8, 3, 48, C), BF16),
+        "spread": pltpu.VMEM((96, C), F32),
+        "by": pltpu.VMEM((8, 96, C), BF16),
+        "joined": pltpu.VMEM((3, 96, C), F32),
+        "hs": pltpu.VMEM((4, 32, 384), BF16),
+        "hr": pltpu.VMEM((2, 2, 32, 384), BF16),
+        "bf": pltpu.VMEM((4, 4, 48, 768), BF16),
+        "wall": pltpu.VMEM((3, C, 512), BF16),
+        "wide": pltpu.VMEM((512, 384), BF16),
+        "q": pltpu.VMEM((6, 4, 4, 48, C), BF16),
+        "k": pltpu.VMEM((6, 768, C), BF16),
+        "v": pltpu.VMEM((6, 768, C), BF16),
+        "g": pltpu.VMEM((2, 4, 4, 48, C), BF16),
+        "rs": pltpu.VMEM((2, 4, 4, 48, C), BF16),
+        "rx": pltpu.VMEM((8, 4, 48, C), BF16),
+        "by_s": dma((8,)),
+        "by_r": dma((8,)),
+        "xy_s": dma((8,)),
+        "xy_r": dma((8,)),
+        "xz_s": dma((8,)),
+        "xz_r": dma((8,)),
+        "xc_s": dma((2,)),
+        "xc_r": dma((2,)),
+        "h_s": dma((4,)),
+        "h_r": dma((2, 2)),
+        "bz_s": dma((4,)),
+        "bz_r": dma((4,)),
+        "bx_s": dma((4, 4)),
+        "bx_r": dma((4, 4)),
+        "rt_s": dma((2, 4, 4)),
+        "rt_r": dma((8, 4)),
+    }
+
+
+def partners1(p):
+    out = []
+    for c in range(2):
+        for z in range(2):
+            for e in range(8):
+                if (c, z, e) != (0, 0, 0):
+                    out.append(p.dev(co=(p.co + c) % 2, zl=(p.zl + z) % 2, y=(p.y + e) % 8))
+    for d in range(1, 4):
+        out.append(p.dev(zh=(p.zh + d) % 4))
+        out.append(p.dev(x=(p.x + d) % 4))
+    return out
+
+
+def phase1(p, ready, src, mask, proj, bias_w, out_w, dst, m):
+    head = 2 * p.zl + p.co
+    copies = []
+
+    def norm_block(b, _):
+        at = pl.multiple_of(b * 144, 16)
+        m["nrm"][b] = layer_norm(src[pl.ds(at, 144), :]).astype(BF16)
+        return 0
+
+    lax.fori_loop(0, 8, norm_block, 0)
+    m["by"][p.y] = local_bias(m["nrm"][...].reshape(1152, C), bias_w[...], m["spread"])
+    ready()
+    for d in range(1, 8):
+        to = (p.y + d) % 8
+        copies.append(
+            send(m["by"].at[p.y], m["by"].at[p.y], m["by_s"].at[d], m["by_r"].at[p.y], p.dev(y=to))
+        )
+    for d in range(1, 8):
+        to = (p.y + d) % 8
+        copies.append(
+            send(
+                m["nrm"].at[to],
+                m["x1f"].at[p.co, p.zl, p.y],
+                m["xy_s"].at[d],
+                m["xy_r"].at[p.y],
+                p.dev(y=to),
+            )
+        )
+    m["x1f"][p.co, p.zl, p.y] = m["nrm"][p.y]
+
+    for a in range(3):
+        first, here = pick(head, 0), pick(head, 32 * a)
+        m["wall"][a, :, 0:128] = dot(proj[:, 0:128], first).astype(BF16)
+        m["wall"][a, :, 128:256] = dot(proj[:, 128:256], first).astype(BF16)
+        m["wall"][a, :, 256:384] = dot(proj[:, 256:384], here).astype(BF16)
+        m["wall"][a, :, 384:512] = dot(proj[:, 384:512], here).astype(BF16)
+    spread_out(out_w, m["wide"])
+
+    for d in range(1, 8):
+        fr = (p.y + d) % 8
+        got(m["by"].at[fr], m["by_r"].at[fr], p.dev(y=fr))
+    join_columns(m["by"], m["joined"])
+    for h in range(HEADS):
+        m["hs"][h] = head_rows(m["joined"], h)
+    m["hr"][p.co, p.zl] = m["hs"][head]
+    for c in range(2):
+        for z in range(2):
+            if (c, z) != (0, 0):
+                co, zl = (p.co + c) % 2, (p.zl + z) % 2
+                copies.append(
+                    send(
+                        m["hs"].at[2 * zl + co],
+                        m["hr"].at[p.co, p.zl],
+                        m["h_s"].at[2 * c + z],
+                        m["h_r"].at[p.co, p.zl],
+                        p.dev(co=co, zl=zl),
+                    )
+                )
+
+    for d in range(8):
+        fr = (p.y + d) % 8
+        block = m["x1f"].at[p.co, p.zl, fr]
+        if d:
+            got(block, m["xy_r"].at[fr], p.dev(y=fr))
+        copies.append(
+            send(block, block, m["xz_s"].at[d], m["xz_r"].at[fr], p.dev(zl=(p.zl + 1) % 2))
+        )
+    half = m["x1f"].at[p.co, p.zl]
+    copies.append(
+        send(half, half, m["xc_s"].at[0], m["xc_r"].at[p.zl], p.dev(co=(p.co + 1) % 2))
+    )
+
+    for c in range(2):
+        for z in range(2):
+            if (c, z) != (0, 0):
+                co, zl = (p.co + c) % 2, (p.zl + z) % 2
+                got(m["hr"].at[co, zl], m["h_r"].at[co, zl], p.dev(co=co, zl=zl))
+    halves = []
+    for z in range(2):
+        rows = [m["hr"][c, z].astype(F32)[0:24] for c in range(2)]
+        halves.append(jnp.concatenate(rows, axis=0))
+    whole = jnp.concatenate(halves, axis=1)
+    m["bf"][p.x, p.zh] = jnp.where(mask[...] > 0, whole, NEG).astype(BF16)
+
+    def to_columns(zh):
+        block = m["bf"].at[p.x, zh]
+        for d in range(1, 4):
+            copies.append(
+                send(
+                    block,
+                    block,
+                    m["bx_s"].at[d, zh],
+                    m["bx_r"].at[p.x, zh],
+                    p.dev(x=(p.x + d) % 4),
+                )
+            )
+
+    mine = m["bf"].at[p.x, p.zh]
+    for d in range(1, 4):
+        copies.append(
+            send(mine, mine, m["bz_s"].at[d], m["bz_r"].at[p.zh], p.dev(zh=(p.zh + d) % 4))
+        )
+    to_columns(p.zh)
+    other = (p.zl + 1) % 2
+    for d in range(8):
+        fr = (p.y + d) % 8
+        got(m["x1f"].at[p.co, other, fr], m["xz_r"].at[fr], p.dev(zl=other))
+    half = m["x1f"].at[p.co, other]
+    copies.append(
+        send(half, half, m["xc_s"].at[1], m["xc_r"].at[other], p.dev(co=(p.co + 1) % 2))
+    )
+    for d in range(1, 4):
+        zh = (p.zh + d) % 4
+        got(m["bf"].at[p.x, zh], m["bz_r"].at[zh], p.dev(zh=zh))
+        to_columns(zh)
+
+    lane = iota((768, C), 1)
+
+    def prepare(t, _):
+        co = (p.co + t) % 2
+
+        @pl.when(t == 1)
+        def _():
+            for zl in range(2):
+                got(m["x1f"].at[co, zl], m["xc_r"].at[zl], p.dev(co=co))
+
+        gate = jnp.zeros((768, C), F32)
+        for a in range(3):
+            rows = m["x1f"][co, :, :, a * 48 : a * 48 + 48, :].reshape(768, C)
+            mixed = dot(rows, m["wall"][a])
+            item = 3 * co + a
+            query = (mixed[:, 0:128] * HD ** (-0.5)).astype(BF16)
+            m["q"][item] = query.reshape(4, 4, 48, C)
+            m["k"][item] = mixed[:, 128:256].astype(BF16)
+            value = jnp.where(lane == 96 + a, 1.0, mixed[:, 256:384])
+            m["v"][item] = value.astype(BF16)
+            gate = gate + mixed[:, 384:512]
+        gate = jnp.where(lane < 96, jax.nn.sigmoid(gate), 0.0)
+        m["g"][co] = gate.astype(BF16).reshape(4, 4, 48, C)
+        return 0
+
+    lax.fori_loop(0, 2, prepare, 0)
+
+    lane = iota((192, C), 1)
+
+    def attend(t, _):
+        s, co = t // 2, t % 2
+        x = (p.x + s + jnp.where(s == 2, 1, 0) - jnp.where(s == 3, 1, 0)) % 4
+
+        @pl.when((s > 0) & (co == 0))
+        def _():
+            for zh in range(4):
+                got(m["bf"].at[x, zh], m["bx_r"].at[x, zh], p.dev(x=x))
+
+        bias = m["bf"][x].reshape(192, 768)
+        out = jnp.zeros((192, C), F32)
+        for a in range(3):
+            item = 3 * co + a
+            query = m["q"][item, :, x].reshape(192, C)
+            scores = dot_nt(query, m["k"][item]) + bias.astype(F32)
+            top = jnp.max(scores, axis=-1, keepdims=True)
+            weights = jnp.exp(scores - top).astype(BF16)
+            out = out + dot(weights, m["v"][item])
+        inv = [1.0 / out[:, 96 + a : 97 + a] for a in range(3)]
+        scale = jnp.where(lane < 32, inv[0], jnp.where(lane < 64, inv[1], inv[2]))
+        gated = out * scale * m["g"][co, :, x].reshape(192, C).astype(F32)
+        m["rs"][co, :, x] = gated.astype(BF16).reshape(4, 48, C)
+        for zh in range(4):
+            zl, y = zh // 2, (zh % 2) * 4 + x
+            self = (co == p.co) & (zl == p.zl) & (y == p.y)
+
+            @pl.when(self)
+            def _():
+                m["rx"][p.y, head] = m["rs"][co, zh, x]
+
+            @pl.when(jnp.logical_not(self))
+            def _():
+                send(
+                    m["rs"].at[co, zh, x],
+                    m["rx"].at[p.y, head],
+                    m["rt_s"].at[co, zh, x],
+                    m["rt_r"].at[p.y, head],
+                    p.dev(co=co, zl=zl, y=y),
+                )
+
+        return 0
+
+    lax.fori_loop(0, 8, attend, 0)
+
+    def take(t, _):
+        y, h = t // 4, t % 4
+        zl, co = h // 2, h % 2
+
+        @pl.when(jnp.logical_not((y == p.y) & (h == head)))
+        def _():
+            got(m["rx"].at[y, h], m["rt_r"].at[y, h], p.dev(co=co, zl=zl, y=y))
+
+        return 0
+
+    lax.fori_loop(0, 32, take, 0)
+
+    def finish(y, _):
+        rows = jnp.concatenate([m["rx"][y, h] for h in range(HEADS)], axis=1)
+        update = dot(rows, m["wide"][...])
+        for a in range(3):
+            at = pl.multiple_of((3 * y + a) * 48, 16)
+            dst[pl.ds(at, 48), :] = src[pl.ds(at, 48), :] + update[:, a * 128 : a * 128 + 128]
+        return 0
+
+    lax.fori_loop(0, 8, finish, 0)
+
+    for copy in copies:
+        copy.wait_send()
+
+    def leave(t, _):
+        co, zh, x = t // 16, (t // 4) % 4, t % 4
+        zl, y = zh // 2, (zh % 2) * 4 + x
+
+        @pl.when(jnp.logical_not((co == p.co) & (zl == p.zl) & (y == p.y)))
+        def _():
+            sent(m["rs"].at[co, zh, x], m["rt_s"].at[co, zh, x], p.dev(co=co, zl=zl, y=y))
+
+        return 0
+
+    lax.fori_loop(0, 32, leave, 0)
+
+
+def kernel1(names, src, mask, proj, bias_w, out_w, dst, *refs):
+    m = dict(zip(names, refs))
+    p = Place()
+    partners = partners1(p)
+    barrier = pltpu.get_barrier_semaphore()
+    for device in partners:
+        pl.semaphore_signal(barrier, inc=1, device_id=device, device_id_type=MESH)
+
+    def ready():
+        pl.semaphore_wait(barrier, len(partners))
+
+    phase1(p, ready, src, mask, proj, bias_w, out_w, dst, m)
+
+
+def call1(pair, mask, proj, bias_w, out_w):
+    scratch = scratch1()
+    scratch["x1f"] = pltpu.VMEM((2, 2, 8, 144, C), BF16)
+    del scratch["x1"]
+    vmem = pl.BlockSpec(memory_space=pltpu.VMEM)
+    return pl.pallas_call(
+        functools.partial(kernel1, tuple(scratch)),
+        out_shape=jax.ShapeDtypeStruct(pair.shape, F32),
+        in_specs=[vmem] * 5,
+        out_specs=vmem,
+        scratch_shapes=list(scratch.values()),
+        compiler_params=pltpu.CompilerParams(
+            collective_id=0, has_side_effects=True, vmem_limit_bytes=48 << 20
+        ),
+        name="start_attention",
+    )(pair, mask, proj, bias_w, out_w)
 
 
 def normalize(field):
@@ -54,32 +469,12 @@
 
 
 def shards(pair, residue_mask, start_proj, start_bias_w, start_out, end_proj, end_bias_w, end_out):
-    rows, cols = (pair.shape[0], pair.shape[1])
+    rows, cols = pair.shape[:2]
+    mask = residue_mask.reshape(1, -1)
+    mid = call1(pair.reshape(rows * cols, C), mask, start_proj, start_bias_w, start_out)
+    pair_mid = mid.reshape(rows, cols, C)
     n_row = lax.axis_size("row")
-    n_col = lax.axis_size("col")
-    group = n_col // HEADS
     quarter = n_row // HEADS
-    normed = normalize(pair)
-    packed = project(normed, start_proj)
-    items = rows // group
-    send = packed.reshape(group, items, cols, 4, HEADS, HD).transpose(4, 0, 1, 2, 3, 5)
-    send = send.reshape(n_col, items, cols, 4 * HD)
-    bias = head_bias(normed, start_bias_w).transpose(2, 0, 1)
-    tall = lax.all_gather(bias, "row", axis=1, tiled=True)
-    bias_send = jnp.repeat(tall, group, axis=0)
-    moved, bias_moved = (
-        lax.all_to_all(send, "col", split_axis=0, concat_axis=2, tiled=True),
-        lax.all_to_all(bias_send, "col", split_axis=0, concat_axis=2, tiled=True),
-    )
-    lanes = moved[0]
-    attended = attend(lanes, bias_moved, residue_mask)
-    back = lax.all_to_all(attended, "col", split_axis=1, concat_axis=0, tiled=True)
-    merged = (
-        back.reshape(HEADS, group, items, cols, HD).transpose(1, 2, 3, 0, 4).reshape(rows * cols, C)
-    )
-    pair_mid = pair + jnp.dot(merged, start_out, preferred_element_type=jnp.float32).reshape(
-        rows, cols, C
-    )
     normed2 = normalize(pair_mid)
     packed2 = project(normed2, end_proj)
     width = cols // quarter

time: 319 us -> 238 us (0.75)
  Pallas kernels: 0 us -> 61.7 us
  blocking collectives: 108 us -> 51.2 us
  waiting for transfers between devices: 67.9 us -> 36.1 us
  starting transfers between devices: 44.6 us -> 23.3 us
  local copies, waits for them, and re-layouts: 58.3 us -> 43.4 us
  matrix products: 21.3 us -> 12.2 us
  other arithmetic: 17.5 us -> 8.5 us
    pallas_call x0 -> x1, Pallas kernels: none -> 61.7 us  [call1(): pl.pallas_call(functools.partial(kernel1, tuple(scratch)), out_shape=jax....]
    all_gather x1 -> x0, blocking collectives: 52.8 us -> none  [shards(): tall = lax.all_gather(bias, 'row', axis=1, tiled=True)]
    all_to_all x3 -> x0, waiting for transfers between devices: 35.9 us -> none  [the longest x1 26.7 us: shards(): lax.all_to_all(bias_send, 'col', split_axis=0, concat_axis=2, tiled=True)]
    all_to_all x3 -> x0, starting transfers between devices: 24.8 us -> none  [the longest x1 9.56 us: shards(): lax.all_to_all(send, 'col', split_axis=0, concat_axis=2, tiled=True)]
    dynamic_slice x24 -> x12, local copies, waits for them, and re-layouts: 13.1 us -> 6.52 us  [attend(): return lax.map(one_item, (lanes, lanes))]
    all_to_all x1, starting transfers between devices: 8.6 us -> 14.2 us  [shards(): lax.all_to_all(send2, 'row', split_axis=0, concat_axis=2, tiled=True)]
    dot_general x12 -> x6, matrix products: 9.9 us -> 6.81 us  [one_item(): jnp.dot(weights, whole[:, 2 * HD:3 * HD], preferred_element_type=jnp.floa...]
    slice x3 -> x2, local copies, waits for them, and re-layouts: 6.79 us -> 6.42 us  [project(): mixed[:, :, 1]]
  transfers between devices with their start and end apart: 5 -> 2, of which waited for: 4 -> 2; matrix products, arithmetic and copies ran while one was open for 1% -> 1% of each run, Pallas kernels for 0% -> 0%
where the time goes in v1:
time: 238 us; the launch traced here: 237 us
  Pallas kernels  61.7 us (26%)
  blocking collectives  51.2 us (22%)
  local copies, waits for them, and re-layouts  43.4 us (18%)
  waiting for transfers between devices  36.1 us (15%)
  starting transfers between devices  23.3 us (10%)
  matrix products  12.2 us (5%)
  other arithmetic  8.5 us (4%)
    pallas_call x1, Pallas kernels, call1(): pl.pallas_call(functools.partial(kernel1, tuple(scratch)), out_shape=jax....  61.7 us
    all_gather x1, blocking collectives, shards(): broad = lax.all_gather(bias2, 'col', axis=1, tiled=True)  31.3 us
    all_to_all x1, waiting for transfers between devices, shards(): lax.all_to_all(bias_send2, 'row', split_axis=0, concat_axis=2, tiled=True)  29.4 us
    all_to_all x1, blocking collectives, shards(): lax.all_to_all(attended2, 'row', split_axis=1, concat_axis=0, tiled=True)  20 us
    all_to_all x1, starting transfers between devices, shards(): lax.all_to_all(send2, 'row', split_axis=0, concat_axis=2, tiled=True)  14.2 us
    all_to_all x1, starting transfers between devices, shards(): lax.all_to_all(bias_send2, 'row', split_axis=0, concat_axis=2, tiled=True)  9.11 us
    dot_general x6, matrix products, one_item(): jnp.dot(weights, whole[:, 2 * HD:3 * HD], preferred_element_type=jnp.floa...  6.81 us
    all_to_all x1, waiting for transfers between devices, shards(): lax.all_to_all(send2, 'row', split_axis=0, concat_axis=2, tiled=True)  6.77 us
  transfers between devices with their start and end apart: 2, of which 2 were waited for; matrix products, arithmetic and copies ran while one was open for 1% of the time, Pallas kernels for 0%

profile of v1, /device:TPU:1, one launch (start us, length us, event | category | flops | bytes accessed | tf_op | source)
XLA Modules:
  0.0 236.8 jit_solution(5615568426526223158)
XLA Ops:
  0.0 0.7 reshape.72.mask
  0.7 0.8 copy.25.bias_w
  1.5 1.1 copy-done.1
  2.6 0.9 copy-done.2
  3.5 0.8 copy-done.3
  4.2 61.7 %start_attention.1 = f32[1152,128]{1,0:T(8,128)S(1)} custom-call(f32[1152,128]{1,0:T(8,128)S(1)} %bitcast.63, s32[1,768]{1,0:T(1,128)S(1)} %reshape.72.mask, bf16[128,512]{1,0:T(8,128)(2,1)S(1)} %copy-done.2, bf16[128,4]{1,0:T(8,128)(2,1)S(1)} %copy.25.bias_w, bf16[128,128]{1,0:T(8,128)(2,1)S(1)} %copy-done.3), custom_call_target="tpu_custom_call" | custom-call | tf_op jit(solution)/shard_map/start_attention/pallas_call | solution.py:413
  66.0 0.2 reduce_sum.27
  66.2 0.4 multiply_reduce_fusion
  66.7 0.4 multiply_convert_fusion
  67.2 1.0 fusion.16
  68.2 1.3 fusion.12
  69.5 1.6 slice.54
  71.1 1.8 copy.29
  72.9 4.8 %copy.28 = bf16[24,48,2,4,32]{4,0,3,2,1:T(8,128)(2,1)S(1)} copy(bf16[24,48,2,4,32]{1,4,3,2,0:T(8,128)(2,1)} %slice.54) | data formatting | bytes 1179648 | tf_op jit(solution)/shard_map/slice | solution.py:439
  77.7 2.8 %copy.27 = bf16[24,48,1,4,32]{4,0,3,1,2:T(8,128)(2,1)} copy(bf16[24,48,1,4,32]{1,4,3,2,0:T(8,128)(2,1)} %get-tuple-element.55) | data formatting | bytes 589824 | tf_op jit(solution)/shard_map/convert.9
  80.5 2.5 %maximum_bitcast_fusion = bf16[4,8,6,24,4,32]{5,3,0,4,2,1:T(8,128)(2,1)S(1)} fusion(bf16[24,8,6,1,4,32]{5,0,4,3,2,1:T(8,128)(2,1)} %bitcast.70, bf16[24,8,6,2,4,32]{5,0,4,3,2,1:T(8,128)(2,1)S(1)} %bitcast.67, bf16[24,8,6,1,4,32]{5,0,4,3,2,1:T(8,128)(2,1)} %bitcast.71), kind=kLoop, calls=%fused_computation.13 | loop fusion | flops 1179648 | bytes 2359296 | tf_op jit(solution)/shard_map/transpose | solution.py:481
  83.0 5.8 %copy.32 = bf16[4,8,6,24,4,32]{5,4,3,2,1,0:T(4,128)(2,1)} copy(bf16[4,8,6,24,4,32]{5,3,0,4,2,1:T(8,128)(2,1)S(1)} %maximum_bitcast_fusion) | data formatting | bytes 2359296 | tf_op jit(solution)/shard_map/transpose | solution.py:481
  88.8 6.5 %reshape.74 = bf16[32,6,24,128]{3,2,1,0:T(8,128)(2,1)} reshape(bf16[4,8,6,24,4,32]{5,4,3,2,1,0:T(4,128)(2,1)} %copy.32) | data formatting | bytes 2359296 | tf_op jit(solution)/shard_map/reshape | solution.py:482
  95.3 14.2 %all-to-all-start = ((bf16[32,6,24,128]{3,2,1,0:T(8,128)(2,1)}), bf16[32,6,24,128]{3,2,1,0:T(8,128)(2,1)S(1)}, u32[]{:S(2)}, u32[]{:S(2)}) async-start(bf16[32,6,24,128]{3,2,1,0:T(8,128)(2,1)} %reshape.74), calls=%async_computation | async-start | bytes 2359296 | tf_op jit(solution)/shard_map/all_to_all | solution.py:487
  109.5 0.2 convolution_convert_fusion
  109.9 31.3 %all_gather.3 = bf16[4,768,24]{2,0,1:T(4,128)(2,1)S(1)} all-gather(bf16[4,48,24]{2,0,1:T(4,128)(2,1)S(1)} %bitcast.76), channel_id=1, replica_groups=mesh['row'=32,'col'=16] {'col'}, dimensions={1}, use_global_device_ids=true | all-gather | bytes 156672 | tf_op jit(solution)/shard_map/all_gather | solution.py:484
  141.2 0.5 copy.35
  141.7 6.8 %all-to-all-done = bf16[32,6,24,128]{3,2,1,0:T(8,128)(2,1)S(1)} async-done(((bf16[32,6,24,128]{3,2,1,0:T(8,128)(2,1)}), bf16[32,6,24,128]{3,2,1,0:T(8,128)(2,1)S(1)}, u32[]{:S(2)}, u32[]{:S(2)}) %all-to-all-start) | async-done | bytes 1179680 | tf_op jit(solution)/shard_map/all_to_all | solution.py:487
  148.4 1.1 broadcast_in_dim.28
  149.5 9.1 %all-to-all-start.1 = ((bf16[32,768,24]{1,2,0:T(8,128)(2,1)}), bf16[32,768,24]{1,2,0:T(8,128)(2,1)}, u32[]{:S(2)}, u32[]{:S(2)}) async-start(bf16[32,768,24]{1,2,0:T(8,128)(2,1)} %bitcast.20), calls=%async_computation.1 | async-start | bytes 2359296 | tf_op jit(solution)/shard_map/all_to_all | solution.py:488
  158.7 1.2 copy.33
  159.9 29.4 %all-to-all-done.1 = bf16[32,768,24]{1,2,0:T(8,128)(2,1)} async-done(((bf16[32,768,24]{1,2,0:T(8,128)(2,1)}), bf16[32,768,24]{1,2,0:T(8,128)(2,1)}, u32[]{:S(2)}, u32[]{:S(2)}) %all-to-all-start.1) | async-done | bytes 1179680 | tf_op jit(solution)/shard_map/all_to_all | solution.py:488
  189.3 1.4 bitcast_convert_fusion
  190.7 18.8 %while.10 = (s32[]{:T(128)}, bf16[6,768,32]{1,2,0:T(8,128)(2,1)}, pred[768]{0:T(1024)(128)(4,1)S(1)}, bf16[6,768,128]{2,1,0:T(8,128)(2,1)}, f32[768,768]{0,1:T(8,128)S(1)}, /*index=5*/s32[]{:T(128)}) while((s32[]{:T(128)}, bf16[6,768,32]{1,2,0:T(8,128)(2,1)}, pred[768]{0:T(1024)(128)(4,1)S(1)}, bf16[6,768,128]{2,1,0:T(8,128)(2,1)}, ...), condition=%wide.region_5.6_spmd, body=%wide.region_2.5_spmd.sunk | while | flops 80288256 | bytes 10487893 | solution.py:468
  190.7 0.9 constant_dynamic-slice_fusion.2
  191.7 0.1 copy.47
  191.8 0.5 fusion.27
  192.4 0.4 fusion.28
  192.7 1.1 fusion.29
  193.9 0.9 constant_dynamic-slice_fusion.2
  195.0 0.5 fusion.27
  195.5 0.4 fusion.28
  195.9 1.1 fusion.29
  197.0 0.9 constant_dynamic-slice_fusion.2
  198.0 0.1 copy.47
  198.1 0.5 fusion.27
  198.7 0.4 fusion.28
  199.0 1.1 fusion.29
  200.2 0.9 constant_dynamic-slice_fusion.2
  201.1 0.1 copy.47
  201.2 0.5 fusion.27
  201.8 0.4 fusion.28
  202.2 1.1 fusion.29
  203.3 0.9 constant_dynamic-slice_fusion.2
  204.4 0.5 fusion.27
  204.9 0.4 fusion.28
  205.3 1.1 fusion.29
  206.4 0.9 constant_dynamic-slice_fusion.2
  207.4 0.1 copy.47
  207.5 0.5 fusion.27
  208.1 0.4 fusion.28
  208.4 1.1 fusion.29
  209.6 1.9 copy.37
  211.5 1.1 reshape.83
  212.7 20.0 %all_to_all.39 = bf16[32,2,2304]{2,1,0:T(2,128)(2,1)S(1)} all-to-all(bf16[32,2,2304]{2,1,0:T(2,128)(2,1)S(1)} %reshape.83), channel_id=1, replica_groups=mesh['row'=32,'col'=16] {'row'}, dimensions={0} | all-to-all | bytes 589824 | tf_op jit(solution)/shard_map/all_to_all | solution.py:492
  232.6 1.0 reshape.84
  233.7 1.5 copy.40
  235.2 0.6 dot_general.28
  235.8 1.0 convolution_add_fusion
  (20 shorter events, 0.7 us)
Async XLA Ops:
  0.0 235.8 %copy-start = (bf16[128,128]{1,0:T(8,128)(2,1)S(1)}, bf16[128,128]{1,0:T(8,128)(2,1)}, u32[]{:S(2)}) copy-start(bf16[128,128]{1,0:T(8,128)(2,1)} %param.17) | copy-start | bytes 98308
  1.5 1.1 copy-start.1
  2.6 0.9 copy-start.2
  3.5 0.8 copy-start.3
  4.2 62.8 %copy-start.4 = (bf16[128,512]{1,0:T(8,128)(2,1)S(1)}, bf16[128,512]{1,0:T(8,128)(2,1)}, u32[]{:S(2)}) copy-start(bf16[128,512]{1,0:T(8,128)(2,1)} %param.15) | copy-start | bytes 393220
  95.3 14.2 %copy-start.6 = (bf16[128,4]{0,1:T(4,128)(2,1)S(1)}, bf16[128,4]{0,1:T(4,128)(2,1)}, u32[]{:S(2)}) copy-start(bf16[128,4]{0,1:T(4,128)(2,1)} %param.16) | copy-start | bytes 3076
  95.3 53.2 %all-to-all-start = ((bf16[32,6,24,128]{3,2,1,0:T(8,128)(2,1)}), bf16[32,6,24,128]{3,2,1,0:T(8,128)(2,1)S(1)}, u32[]{:S(2)}, u32[]{:S(2)}) async-start(bf16[32,6,24,128]{3,2,1,0:T(8,128)(2,1)} %reshape.74), calls=%async_computation | async-start | bytes 2359296 | tf_op jit(solution)/shard_map/all_to_all | solution.py:487
  141.2 17.5 %copy-start.5 = (s32[768]{0:T(1024)S(1)}, s32[768]{0:T(1024)}, u32[]{:S(2)}) copy-start(s32[768]{0:T(1024)} %param.11) | copy-start | bytes 9220
  149.5 39.7 %all-to-all-start.1 = ((bf16[32,768,24]{1,2,0:T(8,128)(2,1)}), bf16[32,768,24]{1,2,0:T(8,128)(2,1)}, u32[]{:S(2)}, u32[]{:S(2)}) async-start(bf16[32,768,24]{1,2,0:T(8,128)(2,1)} %bitcast.20), calls=%async_computation.1 | async-start | bytes 2359296 | tf_op jit(solution)/shard_map/all_to_all | solution.py:488

commit v2 on v1

--- a/solution.py
+++ b/solution.py
@@ -34,6 +34,8 @@
         r, c = lax.axis_index("row"), lax.axis_index("col")
         self.zh, self.x, self.co = r // 8, (r // 2) % 4, r % 2
         self.zl, self.y = c // 8, c % 8
+        self.yl = self.y % 2
+        self.y1 = self.y + 1 - 2 * self.yl
 
     def dev(self, zh=None, x=None, co=None, zl=None, y=None):
         zh = self.zh if zh is None else zh
@@ -117,7 +119,7 @@
     dma = pltpu.SemaphoreType.DMA
     return {
         "nrm": pltpu.VMEM((8, 144, C), BF16),
-        "x1": pltpu.VMEM((2, 2, 8, 3, 48, C), BF16),
+        "x1f": pltpu.VMEM((2, 2, 8, 144, C), BF16),
         "spread": pltpu.VMEM((96, C), F32),
         "by": pltpu.VMEM((8, 96, C), BF16),
         "joined": pltpu.VMEM((3, 96, C), F32),
@@ -151,16 +153,23 @@
     }
 
 
-def partners1(p):
+def partners(p):
     out = []
     for c in range(2):
         for z in range(2):
             for e in range(8):
                 if (c, z, e) != (0, 0, 0):
                     out.append(p.dev(co=(p.co + c) % 2, zl=(p.zl + z) % 2, y=(p.y + e) % 8))
-    for d in range(1, 4):
-        out.append(p.dev(zh=(p.zh + d) % 4))
-        out.append(p.dev(x=(p.x + d) % 4))
+    for a in range(4):
+        for b in range(4):
+            if (a, b) == (0, 0):
+                continue
+            zh, x = (p.zh + a) % 4, (p.x + b) % 4
+            for co in range(2):
+                out.append(p.dev(zh=zh, x=x, co=co))
+                out.append(p.dev(zh=zh, x=x, co=co, y=p.y1))
+    for a in range(1, 4):
+        out.append(p.dev(zh=(p.zh + a) % 4, zl=1 - p.zl))
     return out
 
 
@@ -375,9 +384,6 @@
 
     lax.fori_loop(0, 8, finish, 0)
 
-    for copy in copies:
-        copy.wait_send()
-
     def leave(t, _):
         co, zh, x = t // 16, (t // 4) % 4, t % 4
         zl, y = zh // 2, (zh % 2) * 4 + x
@@ -388,116 +394,362 @@
 
         return 0
 
-    lax.fori_loop(0, 32, leave, 0)
-
-
-def kernel1(names, src, mask, proj, bias_w, out_w, dst, *refs):
-    m = dict(zip(names, refs))
+    def close():
+        for copy in copies:
+            copy.wait_send()
+        lax.fori_loop(0, 32, leave, 0)
+
+    return close
+
+
+def scratch2():
+    dma = pltpu.SemaphoreType.DMA
+    return {
+        "nrm": pltpu.VMEM((8, 144, C), BF16),
+        "nf": pltpu.VMEM((1152, C), F32),
+        "ns": pltpu.VMEM((4, 4, 80, C), BF16),
+        "x2": pltpu.VMEM((2, 2, 4, 4, 80, C), BF16),
+        "xx": pltpu.VMEM((6, 16, 48, C), BF16),
+        "spread": pltpu.VMEM((96, C), F32),
+        "by": pltpu.VMEM((8, 96, C), BF16),
+        "joined": pltpu.VMEM((3, 96, C), F32),
+        "hs": pltpu.VMEM((4, 32, 384), BF16),
+        "hr": pltpu.VMEM((2, 32, 384), BF16),
+        "b2": pltpu.VMEM((4, 4, 2, 48, 384), BF16),
+        "wk": pltpu.VMEM((C, C), BF16),
+        "wt": pltpu.VMEM((C, C), BF16),
+        "wide": pltpu.VMEM((512, 384), BF16),
+        "qt": pltpu.VMEM((6, 2, C, 384), BF16),
+        "k": pltpu.VMEM((6, 768, C), BF16),
+        "vt": pltpu.VMEM((6, 48, 768), BF16),
+        "gt": pltpu.VMEM((6, 2, 32, 384), BF16),
+        "ot": pltpu.VMEM((C, 384), BF16),
+        "tr": pltpu.VMEM((392, C), F32),
+        "rs": pltpu.VMEM((2, 2, 16, 32, C), BF16),
+        "rx": pltpu.VMEM((16, 4, 32, C), BF16),
+        "by_s": dma((8,)),
+        "by_r": dma((8,)),
+        "xa_s": dma((4, 4)),
+        "xa_r": dma((4, 4)),
+        "xy_s": dma((4, 4)),
+        "xy_r": dma((4, 4)),
+        "xc_s": dma((2,)),
+        "xc_r": dma((2,)),
+        "h_s": dma((1,)),
+        "h_r": dma((1,)),
+        "bz_s": dma((4, 2)),
+        "bz_r": dma((4, 2)),
+        "bx_s": dma((4, 4, 2)),
+        "bx_r": dma((4, 4, 2)),
+        "rt_s": dma((2, 2, 16)),
+        "rt_r": dma((16, 4)),
+    }
+
+
+def pick_rows(head, at):
+    row, col = iota((128, 128), 0), iota((128, 128), 1)
+    hit = (row - at == col - 32 * head) & (row >= at) & (row < at + 32)
+    return jnp.where(hit, 1.0, 0.0).astype(BF16)
+
+
+def phase2(p, src, mask, proj, bias_w, out_w, dst, m):
+    head = 2 * p.yl + p.co
+    other = 1 - p.co
+    copies = []
+
+    def norm_block(b, _):
+        at = pl.multiple_of(b * 144, 16)
+        normed = layer_norm(src[pl.ds(at, 144), :]).astype(BF16)
+        m["nrm"][b] = normed
+        m["nf"][pl.ds(at, 144), :] = normed.astype(F32)
+        return 0
+
+    lax.fori_loop(0, 8, norm_block, 0)
+    m["by"][p.y] = local_bias(m["nrm"][...].reshape(1152, C), bias_w[...], m["spread"])
+    for d in range(1, 8):
+        to = (p.y + d) % 8
+        copies.append(
+            send(m["by"].at[p.y], m["by"].at[p.y], m["by_s"].at[d], m["by_r"].at[p.y], p.dev(y=to))
+        )
+
+    for a in range(4):
+        for b in range(4):
+            zh, x = (p.zh + a) % 4, (p.x + b) % 4
+            first = 3 * (zh * 4 + x)
+            rows = [m["nf"][pl.ds(first + i, 24, stride=48), :] for i in range(3)]
+            rows.append(jnp.zeros((8, C), F32))
+            m["ns"][zh, x] = jnp.concatenate(rows, axis=0).astype(BF16)
+            if (a, b) == (0, 0):
+                m["x2"][p.yl, p.co, p.zh, p.x] = m["ns"][zh, x]
+            else:
+                copies.append(
+                    send(
+                        m["ns"].at[zh, x],
+                        m["x2"].at[p.yl, p.co, p.zh, p.x],
+                        m["xa_s"].at[a, b],
+                        m["xa_r"].at[p.zh, p.x],
+                        p.dev(zh=zh, x=x),
+                    )
+                )
+
+    m["wk"][...] = dot(proj[:, 128:256], pick(head, 0)).astype(BF16)
+    wt = dot_nt(pick_rows(head, 0), proj[:, 0:128])
+    wt = wt + dot_nt(pick_rows(head, 32), proj[:, 256:384])
+    wt = wt + dot_nt(pick_rows(head, 64), proj[:, 384:512])
+    m["wt"][...] = wt.astype(BF16)
+    spread_out(out_w, m["wide"])
+
+    for d in range(1, 8):
+        fr = (p.y + d) % 8
+        got(m["by"].at[fr], m["by_r"].at[fr], p.dev(y=fr))
+    join_columns(m["by"], m["joined"])
+    for h in range(HEADS):
+        m["hs"][h] = head_rows(m["joined"], h)
+    m["hr"][p.co] = m["hs"][head]
+    copies.append(
+        send(
+            m["hs"].at[2 * p.yl + other],
+            m["hr"].at[p.co],
+            m["h_s"].at[0],
+            m["h_r"].at[0],
+            p.dev(co=other),
+        )
+    )
+    row, col = iota((48, 768), 0), iota((48, 768), 1)
+    keep = jnp.where(col == row + 48 * (4 * p.zh + p.x), mask[...], 0)
+    keep = jnp.sum(keep.astype(F32), axis=1, keepdims=True)
+    got(m["hr"].at[other], m["h_r"].at[0], p.dev(co=other))
+    whole = jnp.concatenate([m["hr"][c].astype(F32)[0:24] for c in range(2)], axis=0)
+    m["b2"][p.zh, p.x, p.zl] = jnp.where(keep > 0.5, whole, NEG).astype(BF16)
+
+    def to_columns(zh, zl):
+        block = m["b2"].at[zh, p.x, zl]
+        for d in range(1, 4):
+            copies.append(
+                send(
+                    block,
+                    block,
+                    m["bx_s"].at[d, zh, zl],
+                    m["bx_r"].at[p.x, zh, zl],
+                    p.dev(x=(p.x + d) % 4),
+                )
+            )
+
+    mine = m["b2"].at[p.zh, p.x, p.zl]
+    for z in range(2):
+        for a in range(4):
+            if (a, z) != (0, 0):
+                zh, zl = (p.zh + a) % 4, (p.zl + z) % 2
+                copies.append(
+                    send(
+                        mine,
+                        mine,
+                        m["bz_s"].at[a, z],
+                        m["bz_r"].at[p.zh, p.zl],
+                        p.dev(zh=zh, zl=zl),
+                    )
+                )
+    to_columns(p.zh, p.zl)
+
+    for a in range(4):
+        for b in range(4):
+            zh, x = (p.zh + a) % 4, (p.x + b) % 4
+            block = m["x2"].at[p.yl, p.co, zh, x]
+            if (a, b) != (0, 0):
+                got(block, m["xa_r"].at[zh, x], p.dev(zh=zh, x=x))
+            copies.append(
+                send(block, block, m["xy_s"].at[a, b], m["xy_r"].at[zh, x], p.dev(y=p.y1))
+            )
+    part = m["x2"].at[p.yl, p.co]
+    copies.append(send(part, part, m["xc_s"].at[0], m["xc_r"].at[p.yl], p.dev(co=other)))
+
+    for z in range(2):
+        for a in range(4):
+            if (a, z) != (0, 0):
+                zh, zl = (p.zh + a) % 4, (p.zl + z) % 2
+                got(m["b2"].at[zh, p.x, zl], m["bz_r"].at[zh, zl], p.dev(zh=zh, zl=zl))
+                to_columns(zh, zl)
+
+    for a in range(4):
+        for b in range(4):
+            zh, x = (p.zh + a) % 4, (p.x + b) % 4
+            got(m["x2"].at[1 - p.yl, p.co, zh, x], m["xy_r"].at[zh, x], p.dev(y=p.y1))
+    part = m["x2"].at[1 - p.yl, p.co]
+    copies.append(send(part, part, m["xc_s"].at[1], m["xc_r"].at[1 - p.yl], p.dev(co=other)))
+
+    sub = iota((16, 768), 0)
+    ones = jnp.where(sub == 0, 1.0, 0.0)
+
+    def prepare(t, _):
+        yl = (p.yl + t) % 2
+        got(m["x2"].at[yl, other], m["xc_r"].at[yl], p.dev(co=other))
+
+        def arrange(n, _):
+            zh, x = n // 4, n % 4
+            cores = [m["x2"][yl, c, zh, x].astype(F32) for c in range(2)]
+            for b in range(3):
+                rows = [core[24 * b : 24 * b + 24] for core in cores]
+                m["xx"][3 * yl + b, n] = jnp.concatenate(rows, axis=0).astype(BF16)
+            return 0
+
+        lax.fori_loop(0, 16, arrange, 0)
+        for b in range(3):
+            item = 3 * yl + b
+            rows = m["xx"][item].reshape(768, C)
+            m["k"][item] = dot(rows, m["wk"][...]).astype(BF16)
+            mixed = dot_nt(m["wt"][...], rows)
+            query = (mixed * HD ** (-0.5)).astype(BF16)
+            gate = jax.nn.sigmoid(mixed[64:96]).astype(BF16)
+            for z in range(2):
+                m["qt"][item, z] = query[:, 384 * z : 384 * z + 384]
+                m["gt"][item, z] = gate[:, 384 * z : 384 * z + 384]
+            m["vt"][item] = jnp.concatenate([mixed[32:64], ones], axis=0).astype(BF16)
+        return 0
+
+    lax.fori_loop(0, 2, prepare, 0)
+
+    m["ot"][...] = jnp.zeros_like(m["ot"])
+    m["tr"][...] = jnp.zeros_like(m["tr"])
+    eye = jnp.where(iota((128, 128), 0) == iota((128, 128), 1), 1.0, 0.0).astype(BF16)
+
+    def attend(t, _):
+        z, yl = (p.zl + t // 2) % 2, t % 2
+
+        @pl.when(yl == 0)
+        def _():
+            for d in range(1, 4):
+                x = (p.x + d) % 4
+                for zh in range(4):
+                    got(m["b2"].at[zh, x, z], m["bx_r"].at[x, zh, z], p.dev(x=x))
+
+        bias = m["b2"][:, :, z].reshape(768, 384)
+        for b in range(3):
+            item = 3 * yl + b
+            scores = dot(m["k"][item], m["qt"][item, z]) + bias.astype(F32)
+            top = jnp.max(scores, axis=0, keepdims=True)
+            weights = jnp.exp(scores - top).astype(BF16)
+            out = dot(m["vt"][item], weights)
+            gated = out[0:32] / out[32:33] * m["gt"][item, z].astype(F32)
+            m["ot"][32 * b : 32 * b + 32, :] = gated.astype(BF16)
+        for j in range(3):
+            m["tr"][128 * j : 128 * j + 128, :] = dot_nt(eye, m["ot"][:, 128 * j : 128 * j + 128])
+        y = p.y - p.yl + yl
+        for n in range(16):
+            zh, x, co = 2 * z + n // 8, (n // 2) % 4, n % 2
+            m["rs"][z, yl, n] = m["tr"][24 * n : 24 * n + 32, :].astype(BF16)
+            self = (zh == p.zh) & (p.x == x) & (p.co == co) & (yl == p.yl)
+
+            @pl.when(self)
+            def _():
+                m["rx"][4 * p.zh + p.x, head] = m["rs"][z, yl, n]
+
+            @pl.when(jnp.logical_not(self))
+            def _():
+                send(
+                    m["rs"].at[z, yl, n],
+                    m["rx"].at[4 * p.zh + p.x, head],
+                    m["rt_s"].at[z, yl, n],
+                    m["rt_r"].at[4 * p.zh + p.x, head],
+                    p.dev(zh=zh, x=x, co=co, y=y),
+                )
+
+        return 0
+
+    lax.fori_loop(0, 4, attend, 0)
+
+    def take(t, _):
+        s, h = t // 4, t % 4
+        zh, x, yl, co = s // 4, s % 4, h // 2, h % 2
+
+        @pl.when(jnp.logical_not((s == 4 * p.zh + p.x) & (h == head)))
+        def _():
+            got(
+                m["rx"].at[s, h],
+                m["rt_r"].at[s, h],
+                p.dev(zh=zh, x=x, co=co, y=p.y - p.yl + yl),
+            )
+
+        return 0
+
+    lax.fori_loop(0, 64, take, 0)
+
+    def finish(g, _):
+        rows = [m["rx"][pl.ds(4 * g, 4), h].reshape(128, C) for h in range(HEADS)]
+        update = dot(jnp.concatenate(rows, axis=1), m["wide"][...])
+        for s in range(4):
+            for b in range(3):
+                at = pl.ds(3 * (4 * g + s) + b, 24, stride=48)
+                dst[at, :] = src[at, :] + update[32 * s : 32 * s + 24, b * 128 : b * 128 + 128]
+        return 0
+
+    lax.fori_loop(0, 4, finish, 0)
+
+    def leave(t, _):
+        z, yl, n = t // 32, (t // 16) % 2, t % 16
+        zh, x, co = 2 * z + n // 8, (n // 2) % 4, n % 2
+        y = p.y - p.yl + yl
+
+        @pl.when(
+            jnp.logical_not((zh == p.zh) & (x == p.x) & (co == p.co) & (yl == p.yl))
+        )
+        def _():
+            sent(m["rs"].at[z, yl, n], m["rt_s"].at[z, yl, n], p.dev(zh=zh, x=x, co=co, y=y))
+
+        return 0
+
+    def close():
+        for copy in copies:
+            copy.wait_send()
+        lax.fori_loop(0, 64, leave, 0)
+
+    return close
+
+
+def kernel(
+    names1, names2, pair, mask, proj1, bias1_w, out1_w, proj2, bias2_w, out2_w, dst, mid, *refs
+):
+    m1 = dict(zip(names1, refs))
+    m2 = dict(zip(names2, refs[len(names1) :]))
     p = Place()
-    partners = partners1(p)
+    others = partners(p)
     barrier = pltpu.get_barrier_semaphore()
-    for device in partners:
+    for device in others:
         pl.semaphore_signal(barrier, inc=1, device_id=device, device_id_type=MESH)
 
     def ready():
-        pl.semaphore_wait(barrier, len(partners))
-
-    phase1(p, ready, src, mask, proj, bias_w, out_w, dst, m)
-
-
-def call1(pair, mask, proj, bias_w, out_w):
-    scratch = scratch1()
-    scratch["x1f"] = pltpu.VMEM((2, 2, 8, 144, C), BF16)
-    del scratch["x1"]
-    vmem = pl.BlockSpec(memory_space=pltpu.VMEM)
-    return pl.pallas_call(
-        functools.partial(kernel1, tuple(scratch)),
-        out_shape=jax.ShapeDtypeStruct(pair.shape, F32),
-        in_specs=[vmem] * 5,
-        out_specs=vmem,
-        scratch_shapes=list(scratch.values()),
-        compiler_params=pltpu.CompilerParams(
-            collective_id=0, has_side_effects=True, vmem_limit_bytes=48 << 20
-        ),
-        name="start_attention",
-    )(pair, mask, proj, bias_w, out_w)
-
-
-def normalize(field):
-    mean = jnp.mean(field, axis=-1, keepdims=True)
-    centered = field - mean
-    var = jnp.mean(centered * centered, axis=-1, keepdims=True)
-    return (centered * lax.rsqrt(var + 1e-05)).astype(jnp.bfloat16)
-
-
-def project(normed, proj_w):
-    lead = normed.shape[:2]
-    mixed = jnp.dot(normed.reshape(-1, C), proj_w, preferred_element_type=jnp.float32)
-    mixed = mixed.reshape(lead + (4, HEADS, HD))
-    query = mixed[:, :, 0] * HD ** (-0.5)
-    gate = jax.nn.sigmoid(mixed[:, :, 3])
-    return jnp.stack([query, mixed[:, :, 1], mixed[:, :, 2], gate], axis=2).astype(jnp.bfloat16)
-
-
-def head_bias(normed, bias_w):
-    lead = normed.shape[:2]
-    flat = jnp.dot(normed.reshape(-1, C), bias_w, preferred_element_type=jnp.float32)
-    return flat.astype(jnp.bfloat16).reshape(lead + (HEADS,))
-
-
-def attend(lanes, piece, residue_mask):
-    bias = piece[0].astype(jnp.float32)
-    keep = residue_mask > 0
-
-    def one_item(item):
-        selected, whole = item
-        scores = (
-            jnp.einsum(
-                "qd,kd->qk",
-                selected[:, :HD],
-                whole[:, HD : 2 * HD],
-                preferred_element_type=jnp.float32,
-            )
-            + bias
-        )
-        scores = jnp.where(keep[None, :], scores, -1000000000.0)
-        weights = jax.nn.softmax(scores, axis=-1).astype(jnp.bfloat16)
-        out = jnp.dot(weights, whole[:, 2 * HD : 3 * HD], preferred_element_type=jnp.float32)
-        return (out * selected[:, 3 * HD :]).astype(jnp.bfloat16)
-
-    return lax.map(one_item, (lanes, lanes))
+        pl.semaphore_wait(barrier, len(others))
+
+    close1 = phase1(p, ready, pair, mask, proj1, bias1_w, out1_w, mid, m1)
+    close2 = phase2(p, mid, mask, proj2, bias2_w, out2_w, dst, m2)
+    close1()
+    close2()
 
 
 def shards(pair, residue_mask, start_proj, start_bias_w, start_out, end_proj, end_bias_w, end_out):
     rows, cols = pair.shape[:2]
-    mask = residue_mask.reshape(1, -1)
-    mid = call1(pair.reshape(rows * cols, C), mask, start_proj, start_bias_w, start_out)
-    pair_mid = mid.reshape(rows, cols, C)
-    n_row = lax.axis_size("row")
-    quarter = n_row // HEADS
-    normed2 = normalize(pair_mid)
-    packed2 = project(normed2, end_proj)
-    width = cols // quarter
-    send2 = packed2.reshape(rows, quarter, width, 4, HEADS, HD).transpose(4, 1, 2, 0, 3, 5)
-    send2 = send2.reshape(n_row, width, rows, 4 * HD)
-    bias2 = head_bias(normed2, end_bias_w).transpose(2, 1, 0)
-    broad = lax.all_gather(bias2, "col", axis=1, tiled=True)
-    bias_send2 = jnp.repeat(broad, quarter, axis=0)
-    moved2, bias_moved2 = (
-        lax.all_to_all(send2, "row", split_axis=0, concat_axis=2, tiled=True),
-        lax.all_to_all(bias_send2, "row", split_axis=0, concat_axis=2, tiled=True),
+    one, two = scratch1(), scratch2()
+    vmem = pl.BlockSpec(memory_space=pltpu.VMEM)
+    out = pl.pallas_call(
+        functools.partial(kernel, tuple(one), tuple(two)),
+        out_shape=jax.ShapeDtypeStruct((rows * cols, C), F32),
+        in_specs=[vmem] * 8,
+        out_specs=vmem,
+        scratch_shapes=[pltpu.VMEM((rows * cols, C), F32)] + list(one.values()) + list(two.values()),
+        compiler_params=pltpu.CompilerParams(
+            collective_id=0, has_side_effects=True, vmem_limit_bytes=56 << 20
+        ),
+        name="triangle_attention",
+    )(
+        pair.reshape(rows * cols, C),
+        residue_mask.reshape(1, -1),
+        start_proj,
+        start_bias_w,
+        start_out,
+        end_proj,
+        end_bias_w,
+        end_out,
     )
-    lanes2 = moved2[0]
-    attended2 = attend(lanes2, bias_moved2, residue_mask)
-    back2 = lax.all_to_all(attended2, "row", split_axis=1, concat_axis=0, tiled=True)
-    merged2 = (
-        back2.reshape(HEADS, quarter, width, rows, HD)
-        .transpose(3, 1, 2, 0, 4)
-        .reshape(rows * cols, C)
-    )
-    return pair_mid + jnp.dot(merged2, end_out, preferred_element_type=jnp.float32).reshape(
-        rows, cols, C
-    )
+    return out.reshape(rows, cols, C)
 
 
 def solution(mesh):

time: 238 us -> 125 us (0.53)
  the two profiles are of different devices: /device:TPU:1 before, /device:TPU:127 now
where the time goes in v2:
time: 125 us; the launch traced here: 124 us
  Pallas kernels  120 us (96%)
  local copies, waits for them, and re-layouts  4.66 us (4%)
    pallas_call x1, Pallas kernels, shards(): pl.pallas_call(functools.partial(kernel, tuple(one), tuple(two)), out_sha...  120 us
    unnamed x7, local copies, waits for them, and re-layouts  3.38 us

profile of v2, /device:TPU:127, one launch (start us, length us, event | category | flops | bytes accessed | tf_op | source)
XLA Modules:
  0.0 124.5 jit_solution(2611775775670966530)
XLA Ops:
  0.0 0.0 copy-start
  0.0 1.3 %reshape.10.mask = s32[1,768]{1,0:T(1,128)} reshape(s32[768]{0:T(1024)} %param.9) | data formatting | bytes 6144 | tf_op jit(solution)/shard_map/reshape | solution.py:744
  1.3 0.0 copy-done
  1.3 0.0 copy-start.1
  1.3 0.7 copy.9.bias1_w
  2.0 0.0 copy-done.1
  2.0 0.7 copy.10.bias2_w
  2.7 119.8 %triangle_attention.1 = f32[1152,128]{1,0:T(8,128)} custom-call(f32[1152,128]{1,0:T(8,128)} %bitcast.3, s32[1,768]{1,0:T(1,128)} %reshape.10.mask, bf16[128,512]{1,0:T(8,128)(2,1)} %proj1.1, bf16[128,4]{1,0:T(8,128)(2,1)} %copy.9.bias1_w, bf16[128,128]{1,0:T(8,128)(2,1)} %out1_w.1, bf16[128,512]{1,0:T(8,128)(2,1)} %proj2.1, bf16[128,4]{1,0:T(8,128)(2,1)} %copy.10.bias2_w, ...), custom_call_target="tpu_custom_call" | custom-call | tf_op jit(solution)/shard_map/triangle_attention/pallas_call | solution.py:732
  122.5 1.9 %copy.12 = f32[24,48,128]{2,1,0:T(8,128)} copy(f32[24,48,128]{2,1,0:T(8,128)} %bitcast.2) | data formatting | bytes 1179648
Async XLA Ops:
  0.0 1.3 %copy-start = (bf16[128,4]{0,1:T(4,128)(2,1)S(1)}, bf16[128,4]{0,1:T(4,128)(2,1)}, u32[]{:S(2)}) copy-start(bf16[128,4]{0,1:T(4,128)(2,1)} %param.11) | copy-start | bytes 3076
  1.3 0.7 copy-start.1

commit v3 on v2

--- a/solution.py
+++ b/solution.py
@@ -73,28 +73,42 @@
     return centered * lax.rsqrt(var + 1e-05)
 
 
-def local_bias(normed, bias_w, spread):
-    flat = lax.dot_general(bias_w, normed, (((0,), (1,)), ((), ())), preferred_element_type=F32)
+def local_bias(normed, bias_w, spread, heads):
+    flat = dot_nt(bias_w, normed)
     spread[...] = jnp.zeros_like(spread)
     for r in range(24):
-        spread[4 * r : 4 * r + 4, 0:48] = flat[:, 48 * r : 48 * r + 48]
-    return spread[...].astype(BF16)
-
-
-def join_columns(blocks, joined):
-    total = None
-    for b in range(8):
-        lane, col = iota((128, 384), 0), iota((128, 384), 1)
-        place = jnp.where((col == lane + 48 * b) & (lane < 48), 1.0, 0.0).astype(BF16)
-        part = dot(blocks[b], place)
-        total = part if total is None else total + part
-    for j in range(3):
-        joined[j] = total[:, 128 * j : 128 * j + 128]
-
-
-def head_rows(joined, h):
-    rows = jnp.concatenate([joined[j, pl.ds(h, 24, stride=4), :] for j in range(3)], axis=1)
-    return jnp.concatenate([rows, jnp.zeros((8, 384), F32)], axis=0).astype(BF16)
+        row, lane = (r, 0) if r < 8 else (r - 8, 0 if r >= 16 else 64)
+        spread[4 * row : 4 * row + 4, lane : lane + 48] = flat[:, 48 * r : 48 * r + 48]
+    for h in range(HEADS):
+        heads[h] = spread[pl.ds(h, 16, stride=4), :].astype(BF16)
+
+
+def join_columns(blocks):
+    lane = iota(blocks[0].shape, 1)
+    parts = []
+    for first in (0, 64):
+        tiles = [jnp.zeros(blocks[0].shape, F32) for _ in range(3)]
+        for b, block in enumerate(blocks):
+            tile, at = (48 * b) // 128, (48 * b) % 128
+            piece = jnp.where((lane >= first) & (lane < first + 48), block, 0.0)
+            if (at - first) % 128:
+                piece = pltpu.roll(piece, (at - first) % 128, 1)
+            if at + 48 <= 128:
+                tiles[tile] = tiles[tile] + piece
+            else:
+                tiles[tile] = tiles[tile] + jnp.where(lane >= at, piece, 0.0)
+                tiles[tile + 1] = tiles[tile + 1] + jnp.where(lane < at, piece, 0.0)
+        parts.append(tiles)
+    joined = []
+    for base in range(0, blocks[0].shape[0], 16):
+        near, far = slice(base, base + 8), slice(base + 8, base + 16)
+        joined.append(
+            [
+                jnp.concatenate([a[near], b[near], a[far]], axis=0)
+                for a, b in zip(parts[0], parts[1])
+            ]
+        )
+    return joined
 
 
 def pick(head, at):
@@ -112,7 +126,8 @@
             ]
 
 
-STEP = (0, 1, 3, 2)
+NEAR = (0, 1, 3, 2)
+FAR = (4, 3, 5, 2, 6, 1, 7, 0)
 
 
 def scratch1():
@@ -120,11 +135,9 @@
     return {
         "nrm": pltpu.VMEM((8, 144, C), BF16),
         "x1f": pltpu.VMEM((2, 2, 8, 144, C), BF16),
-        "spread": pltpu.VMEM((96, C), F32),
-        "by": pltpu.VMEM((8, 96, C), BF16),
-        "joined": pltpu.VMEM((3, 96, C), F32),
-        "hs": pltpu.VMEM((4, 32, 384), BF16),
-        "hr": pltpu.VMEM((2, 2, 32, 384), BF16),
+        "spread": pltpu.VMEM((64, C), F32),
+        "hs": pltpu.VMEM((4, 16, C), BF16),
+        "by": pltpu.VMEM((2, 2, 8, 16, C), BF16),
         "bf": pltpu.VMEM((4, 4, 48, 768), BF16),
         "wall": pltpu.VMEM((3, C, 512), BF16),
         "wide": pltpu.VMEM((512, 384), BF16),
@@ -134,16 +147,14 @@
         "g": pltpu.VMEM((2, 4, 4, 48, C), BF16),
         "rs": pltpu.VMEM((2, 4, 4, 48, C), BF16),
         "rx": pltpu.VMEM((8, 4, 48, C), BF16),
-        "by_s": dma((8,)),
-        "by_r": dma((8,)),
+        "by_s": dma((2, 2, 8)),
+        "by_r": dma((2, 2, 8)),
         "xy_s": dma((8,)),
         "xy_r": dma((8,)),
         "xz_s": dma((8,)),
         "xz_r": dma((8,)),
         "xc_s": dma((2,)),
         "xc_r": dma((2,)),
-        "h_s": dma((4,)),
-        "h_r": dma((2, 2)),
         "bz_s": dma((4,)),
         "bz_r": dma((4,)),
         "bx_s": dma((4, 4)),
@@ -173,7 +184,7 @@
     return out
 
 
-def phase1(p, ready, src, mask, proj, bias_w, out_w, dst, m):
+def phase1(p, ready, src, mask, proj, bias_w, out_w, dst, nrm, nf, m):
     head = 2 * p.zl + p.co
     copies = []
 
@@ -183,14 +194,24 @@
         return 0
 
     lax.fori_loop(0, 8, norm_block, 0)
-    m["by"][p.y] = local_bias(m["nrm"][...].reshape(1152, C), bias_w[...], m["spread"])
+    local_bias(m["nrm"][...].reshape(1152, C), bias_w[...], m["spread"], m["hs"])
     ready()
-    for d in range(1, 8):
-        to = (p.y + d) % 8
-        copies.append(
-            send(m["by"].at[p.y], m["by"].at[p.y], m["by_s"].at[d], m["by_r"].at[p.y], p.dev(y=to))
-        )
-    for d in range(1, 8):
+    m["by"][p.co, p.zl, p.y] = m["hs"][head]
+    for e in FAR:
+        for c in range(2):
+            for z in range(2):
+                if (c, z, e) != (0, 0, 0):
+                    co, zl, y = (p.co + c) % 2, (p.zl + z) % 2, (p.y + e) % 8
+                    copies.append(
+                        send(
+                            m["hs"].at[2 * zl + co],
+                            m["by"].at[p.co, p.zl, p.y],
+                            m["by_s"].at[c, z, e],
+                            m["by_r"].at[p.co, p.zl, p.y],
+                            p.dev(co=co, zl=zl, y=y),
+                        )
+                    )
+    for d in FAR[:7]:
         to = (p.y + d) % 8
         copies.append(
             send(
@@ -211,27 +232,42 @@
         m["wall"][a, :, 384:512] = dot(proj[:, 384:512], here).astype(BF16)
     spread_out(out_w, m["wide"])
 
-    for d in range(1, 8):
-        fr = (p.y + d) % 8
-        got(m["by"].at[fr], m["by_r"].at[fr], p.dev(y=fr))
-    join_columns(m["by"], m["joined"])
-    for h in range(HEADS):
-        m["hs"][h] = head_rows(m["joined"], h)
-    m["hr"][p.co, p.zl] = m["hs"][head]
-    for c in range(2):
-        for z in range(2):
-            if (c, z) != (0, 0):
-                co, zl = (p.co + c) % 2, (p.zl + z) % 2
-                copies.append(
-                    send(
-                        m["hs"].at[2 * zl + co],
-                        m["hr"].at[p.co, p.zl],
-                        m["h_s"].at[2 * c + z],
-                        m["h_r"].at[p.co, p.zl],
-                        p.dev(co=co, zl=zl),
-                    )
+    for e in FAR:
+        for c in range(2):
+            for z in range(2):
+                if (c, z, e) != (0, 0, 0):
+                    co, zl, y = (p.co + c) % 2, (p.zl + z) % 2, (p.y + e) % 8
+                    got(m["by"].at[co, zl, y], m["by_r"].at[co, zl, y], p.dev(co=co, zl=zl, y=y))
+    joined = join_columns([m["by"][:, :, y].reshape(64, C).astype(F32) for y in range(8)])
+    whole = jnp.concatenate(
+        [
+            jnp.concatenate([joined[z][j], joined[2 + z][j]], axis=0)
+            for z in range(2)
+            for j in range(3)
+        ],
+        axis=1,
+    )
+    m["bf"][p.x, p.zh] = jnp.where(mask[...].reshape(1, 768) > 0, whole, NEG).astype(BF16)
+
+    def to_columns(zh):
+        block = m["bf"].at[p.x, zh]
+        for d in NEAR[1:]:
+            copies.append(
+                send(
+                    block,
+                    block,
+                    m["bx_s"].at[d, zh],
+                    m["bx_r"].at[p.x, zh],
+                    p.dev(x=(p.x + d) % 4),
                 )
-
+            )
+
+    mine = m["bf"].at[p.x, p.zh]
+    for d in NEAR[1:]:
+        copies.append(
+            send(mine, mine, m["bz_s"].at[d], m["bz_r"].at[p.zh], p.dev(zh=(p.zh + d) % 4))
+        )
+    to_columns(p.zh)
     for d in range(8):
         fr = (p.y + d) % 8
         block = m["x1f"].at[p.co, p.zl, fr]
@@ -245,37 +281,10 @@
         send(half, half, m["xc_s"].at[0], m["xc_r"].at[p.zl], p.dev(co=(p.co + 1) % 2))
     )
 
-    for c in range(2):
-        for z in range(2):
-            if (c, z) != (0, 0):
-                co, zl = (p.co + c) % 2, (p.zl + z) % 2
-                got(m["hr"].at[co, zl], m["h_r"].at[co, zl], p.dev(co=co, zl=zl))
-    halves = []
-    for z in range(2):
-        rows = [m["hr"][c, z].astype(F32)[0:24] for c in range(2)]
-        halves.append(jnp.concatenate(rows, axis=0))
-    whole = jnp.concatenate(halves, axis=1)
-    m["bf"][p.x, p.zh] = jnp.where(mask[...] > 0, whole, NEG).astype(BF16)
-
-    def to_columns(zh):
-        block = m["bf"].at[p.x, zh]
-        for d in range(1, 4):
-            copies.append(
-                send(
-                    block,
-                    block,
-                    m["bx_s"].at[d, zh],
-                    m["bx_r"].at[p.x, zh],
-                    p.dev(x=(p.x + d) % 4),
-                )
-            )
-
-    mine = m["bf"].at[p.x, p.zh]
-    for d in range(1, 4):
-        copies.append(
-            send(mine, mine, m["bz_s"].at[d], m["bz_r"].at[p.zh], p.dev(zh=(p.zh + d) % 4))
-        )
-    to_columns(p.zh)
+    for d in NEAR[1:]:
+        zh = (p.zh + d) % 4
+        got(m["bf"].at[p.x, zh], m["bz_r"].at[zh], p.dev(zh=zh))
+        to_columns(zh)
     other = (p.zl + 1) % 2
     for d in range(8):
         fr = (p.y + d) % 8
@@ -284,10 +293,6 @@
     copies.append(
         send(half, half, m["xc_s"].at[1], m["xc_r"].at[other], p.dev(co=(p.co + 1) % 2))
     )
-    for d in range(1, 4):
-        zh = (p.zh + d) % 4
-        got(m["bf"].at[p.x, zh], m["bz_r"].at[zh], p.dev(zh=zh))
-        to_columns(zh)
 
     lane = iota((768, C), 1)
 
@@ -362,24 +367,22 @@
 
     lax.fori_loop(0, 8, attend, 0)
 
-    def take(t, _):
-        y, h = t // 4, t % 4
-        zl, co = h // 2, h % 2
-
-        @pl.when(jnp.logical_not((y == p.y) & (h == head)))
-        def _():
-            got(m["rx"].at[y, h], m["rt_r"].at[y, h], p.dev(co=co, zl=zl, y=y))
-
-        return 0
-
-    lax.fori_loop(0, 32, take, 0)
-
     def finish(y, _):
+        for h in range(HEADS):
+
+            @pl.when(jnp.logical_not((y == p.y) & (h == head)))
+            def _():
+                got(m["rx"].at[y, h], m["rt_r"].at[y, h], p.dev(co=h % 2, zl=h // 2, y=y))
+
         rows = jnp.concatenate([m["rx"][y, h] for h in range(HEADS)], axis=1)
         update = dot(rows, m["wide"][...])
         for a in range(3):
             at = pl.multiple_of((3 * y + a) * 48, 16)
-            dst[pl.ds(at, 48), :] = src[pl.ds(at, 48), :] + update[:, a * 128 : a * 128 + 128]
+            mid = src[pl.ds(at, 48), :] + update[:, a * 128 : a * 128 + 128]
+            dst[pl.ds(at, 48), :] = mid
+            normed = layer_norm(mid).astype(BF16)
+            nrm[pl.ds(at, 48), :] = normed
+            nf[pl.ds(at, 48), :] = normed.astype(F32)
         return 0
 
     lax.fori_loop(0, 8, finish, 0)
@@ -405,16 +408,14 @@
 def scratch2():
     dma = pltpu.SemaphoreType.DMA
     return {
-        "nrm": pltpu.VMEM((8, 144, C), BF16),
+        "nrm": pltpu.VMEM((1152, C), BF16),
         "nf": pltpu.VMEM((1152, C), F32),
         "ns": pltpu.VMEM((4, 4, 80, C), BF16),
         "x2": pltpu.VMEM((2, 2, 4, 4, 80, C), BF16),
         "xx": pltpu.VMEM((6, 16, 48, C), BF16),
-        "spread": pltpu.VMEM((96, C), F32),
-        "by": pltpu.VMEM((8, 96, C), BF16),
-        "joined": pltpu.VMEM((3, 96, C), F32),
-        "hs": pltpu.VMEM((4, 32, 384), BF16),
-        "hr": pltpu.VMEM((2, 32, 384), BF16),
+        "spread": pltpu.VMEM((64, C), F32),
+        "hs": pltpu.VMEM((4, 16, C), BF16),
+        "by": pltpu.VMEM((2, 8, 16, C), BF16),
         "b2": pltpu.VMEM((4, 4, 2, 48, 384), BF16),
         "wk": pltpu.VMEM((C, C), BF16),
         "wt": pltpu.VMEM((C, C), BF16),
@@ -424,25 +425,25 @@
         "vt": pltpu.VMEM((6, 48, 768), BF16),
         "gt": pltpu.VMEM((6, 2, 32, 384), BF16),
         "ot": pltpu.VMEM((C, 384), BF16),
-        "tr": pltpu.VMEM((392, C), F32),
-        "rs": pltpu.VMEM((2, 2, 16, 32, C), BF16),
-        "rx": pltpu.VMEM((16, 4, 32, C), BF16),
-        "by_s": dma((8,)),
-        "by_r": dma((8,)),
+        "tr": pltpu.VMEM((384, C), F32),
+        "rs": pltpu.VMEM((2, 2, 8, 48, C), BF16),
+        "rx": pltpu.VMEM((2, 4, 4, 2, 48, C), BF16),
+        "by_s": dma((2, 8)),
+        "by_r": dma((2, 8)),
         "xa_s": dma((4, 4)),
         "xa_r": dma((4, 4)),
         "xy_s": dma((4, 4)),
         "xy_r": dma((4, 4)),
         "xc_s": dma((2,)),
         "xc_r": dma((2,)),
-        "h_s": dma((1,)),
-        "h_r": dma((1,)),
         "bz_s": dma((4, 2)),
         "bz_r": dma((4, 2)),
         "bx_s": dma((4, 4, 2)),
         "bx_r": dma((4, 4, 2)),
-        "rt_s": dma((2, 2, 16)),
-        "rt_r": dma((16, 4)),
+        "rt_s": dma((2, 2, 8)),
+        "rt_r": dma((4, 4, 2)),
+        "rc_s": dma((4,)),
+        "rc_r": dma((4,)),
     }
 
 
@@ -457,23 +458,24 @@
     other = 1 - p.co
     copies = []
 
-    def norm_block(b, _):
-        at = pl.multiple_of(b * 144, 16)
-        normed = layer_norm(src[pl.ds(at, 144), :]).astype(BF16)
-        m["nrm"][b] = normed
-        m["nf"][pl.ds(at, 144), :] = normed.astype(F32)
-        return 0
-
-    lax.fori_loop(0, 8, norm_block, 0)
-    m["by"][p.y] = local_bias(m["nrm"][...].reshape(1152, C), bias_w[...], m["spread"])
-    for d in range(1, 8):
-        to = (p.y + d) % 8
-        copies.append(
-            send(m["by"].at[p.y], m["by"].at[p.y], m["by_s"].at[d], m["by_r"].at[p.y], p.dev(y=to))
-        )
-
-    for a in range(4):
-        for b in range(4):
+    local_bias(m["nrm"][...], bias_w[...], m["spread"], m["hs"])
+    m["by"][p.co, p.y] = m["hs"][head]
+    for e in FAR:
+        for c in range(2):
+            if (c, e) != (0, 0):
+                co, y = (p.co + c) % 2, (p.y + e) % 8
+                copies.append(
+                    send(
+                        m["hs"].at[2 * (y % 2) + co],
+                        m["by"].at[p.co, p.y],
+                        m["by_s"].at[c, e],
+                        m["by_r"].at[p.co, p.y],
+                        p.dev(co=co, y=y),
+                    )
+                )
+
+    for a in (2, 1, 3, 0):
+        for b in (2, 1, 3, 0):
             zh, x = (p.zh + a) % 4, (p.x + b) % 4
             first = 3 * (zh * 4 + x)
             rows = [m["nf"][pl.ds(first + i, 24, stride=48), :] for i in range(3)]
@@ -499,32 +501,23 @@
     m["wt"][...] = wt.astype(BF16)
     spread_out(out_w, m["wide"])
 
-    for d in range(1, 8):
-        fr = (p.y + d) % 8
-        got(m["by"].at[fr], m["by_r"].at[fr], p.dev(y=fr))
-    join_columns(m["by"], m["joined"])
-    for h in range(HEADS):
-        m["hs"][h] = head_rows(m["joined"], h)
-    m["hr"][p.co] = m["hs"][head]
-    copies.append(
-        send(
-            m["hs"].at[2 * p.yl + other],
-            m["hr"].at[p.co],
-            m["h_s"].at[0],
-            m["h_r"].at[0],
-            p.dev(co=other),
-        )
+    row, col = iota((48, 768), 0), iota((48, 768), 1)
+    keep = jnp.where(col == row + 48 * (4 * p.zh + p.x), mask[...].reshape(1, 768), 0)
+    keep = jnp.sum(keep.astype(F32), axis=1, keepdims=True)
+    for e in FAR:
+        for c in range(2):
+            if (c, e) != (0, 0):
+                co, y = (p.co + c) % 2, (p.y + e) % 8
+                got(m["by"].at[co, y], m["by_r"].at[co, y], p.dev(co=co, y=y))
+    joined = join_columns([m["by"][:, y].reshape(32, C).astype(F32) for y in range(8)])
+    whole = jnp.concatenate(
+        [jnp.concatenate([joined[0][j], joined[1][j]], axis=0) for j in range(3)], axis=1
     )
-    row, col = iota((48, 768), 0), iota((48, 768), 1)
-    keep = jnp.where(col == row + 48 * (4 * p.zh + p.x), mask[...], 0)
-    keep = jnp.sum(keep.astype(F32), axis=1, keepdims=True)
-    got(m["hr"].at[other], m["h_r"].at[0], p.dev(co=other))
-    whole = jnp.concatenate([m["hr"][c].astype(F32)[0:24] for c in range(2)], axis=0)
     m["b2"][p.zh, p.x, p.zl] = jnp.where(keep > 0.5, whole, NEG).astype(BF16)
 
     def to_columns(zh, zl):
         block = m["b2"].at[zh, p.x, zl]
-        for d in range(1, 4):
+        for d in NEAR[1:]:
             copies.append(
                 send(
                     block,
@@ -537,7 +530,7 @@
 
     mine = m["b2"].at[p.zh, p.x, p.zl]
     for z in range(2):
-        for a in range(4):
+        for a in NEAR:
             if (a, z) != (0, 0):
                 zh, zl = (p.zh + a) % 4, (p.zl + z) % 2
                 copies.append(
@@ -551,8 +544,8 @@
                 )
     to_columns(p.zh, p.zl)
 
-    for a in range(4):
-        for b in range(4):
+    for a in NEAR:
+        for b in NEAR:
             zh, x = (p.zh + a) % 4, (p.x + b) % 4
             block = m["x2"].at[p.yl, p.co, zh, x]
             if (a, b) != (0, 0):
@@ -564,14 +557,14 @@
     copies.append(send(part, part, m["xc_s"].at[0], m["xc_r"].at[p.yl], p.dev(co=other)))
 
     for z in range(2):
-        for a in range(4):
+        for a in NEAR:
             if (a, z) != (0, 0):
                 zh, zl = (p.zh + a) % 4, (p.zl + z) % 2
                 got(m["b2"].at[zh, p.x, zl], m["bz_r"].at[zh, zl], p.dev(zh=zh, zl=zl))
                 to_columns(zh, zl)
 
-    for a in range(4):
-        for b in range(4):
+    for a in NEAR:
+        for b in NEAR:
             zh, x = (p.zh + a) % 4, (p.x + b) % 4
             got(m["x2"].at[1 - p.yl, p.co, zh, x], m["xy_r"].at[zh, x], p.dev(y=p.y1))
     part = m["x2"].at[1 - p.yl, p.co]
@@ -609,7 +602,6 @@
     lax.fori_loop(0, 2, prepare, 0)
 
     m["ot"][...] = jnp.zeros_like(m["ot"])
-    m["tr"][...] = jnp.zeros_like(m["tr"])
     eye = jnp.where(iota((128, 128), 0) == iota((128, 128), 1), 1.0, 0.0).astype(BF16)
 
     def attend(t, _):
@@ -634,73 +626,74 @@
         for j in range(3):
             m["tr"][128 * j : 128 * j + 128, :] = dot_nt(eye, m["ot"][:, 128 * j : 128 * j + 128])
         y = p.y - p.yl + yl
-        for n in range(16):
-            zh, x, co = 2 * z + n // 8, (n // 2) % 4, n % 2
-            m["rs"][z, yl, n] = m["tr"][24 * n : 24 * n + 32, :].astype(BF16)
-            self = (zh == p.zh) & (p.x == x) & (p.co == co) & (yl == p.yl)
+        for n in range(8):
+            zh, x = 2 * z + n // 4, n % 4
+            m["rs"][z, yl, n] = m["tr"][48 * n : 48 * n + 48, :].astype(BF16)
+            self = (zh == p.zh) & (p.x == x) & (yl == p.yl)
 
             @pl.when(self)
             def _():
-                m["rx"][4 * p.zh + p.x, head] = m["rs"][z, yl, n]
+                m["rx"][p.co, p.zh, p.x, p.yl] = m["rs"][z, yl, n]
 
             @pl.when(jnp.logical_not(self))
             def _():
                 send(
                     m["rs"].at[z, yl, n],
-                    m["rx"].at[4 * p.zh + p.x, head],
+                    m["rx"].at[p.co, p.zh, p.x, p.yl],
                     m["rt_s"].at[z, yl, n],
-                    m["rt_r"].at[4 * p.zh + p.x, head],
-                    p.dev(zh=zh, x=x, co=co, y=y),
+                    m["rt_r"].at[p.zh, p.x, p.yl],
+                    p.dev(zh=zh, x=x, y=y),
                 )
 
         return 0
 
     lax.fori_loop(0, 4, attend, 0)
 
-    def take(t, _):
-        s, h = t // 4, t % 4
-        zh, x, yl, co = s // 4, s % 4, h // 2, h % 2
-
-        @pl.when(jnp.logical_not((s == 4 * p.zh + p.x) & (h == head)))
+    for d in NEAR:
+        zh = (p.zh + d) % 4
+        for x in range(4):
+            for yl in range(2):
+
+                @pl.when(jnp.logical_not((zh == p.zh) & (x == p.x) & (yl == p.yl)))
+                def _():
+                    got(
+                        m["rx"].at[p.co, zh, x, yl],
+                        m["rt_r"].at[zh, x, yl],
+                        p.dev(zh=zh, x=x, y=p.y - p.yl + yl),
+                    )
+
+        part = m["rx"].at[p.co, zh]
+        copies.append(send(part, part, m["rc_s"].at[d], m["rc_r"].at[zh], p.dev(co=other)))
+
+    def finish(t, _):
+        zh = (p.zh + t + jnp.where(t == 2, 1, 0) - jnp.where(t == 3, 1, 0)) % 4
+        got(m["rx"].at[other, zh], m["rc_r"].at[zh], p.dev(co=other))
+        rows = [m["rx"][h % 2, zh, :, h // 2].reshape(192, C) for h in range(HEADS)]
+        update = dot(jnp.concatenate(rows, axis=1), m["wide"][...])
+        for x in range(4):
+            for b in range(3):
+                chip = update[48 * x : 48 * x + 48, b * 128 : b * 128 + 128]
+                at = pl.ds(3 * (4 * zh + x) + b, 24, stride=48)
+                dst[at, :] = src[at, :] + jnp.where(p.co == 0, chip[0:24], chip[24:48])
+        return 0
+
+    lax.fori_loop(0, 4, finish, 0)
+
+    def leave(t, _):
+        z, yl, n = t // 16, (t // 8) % 2, t % 8
+        zh, x = 2 * z + n // 4, n % 4
+        y = p.y - p.yl + yl
+
+        @pl.when(jnp.logical_not((zh == p.zh) & (x == p.x) & (yl == p.yl)))
         def _():
-            got(
-                m["rx"].at[s, h],
-                m["rt_r"].at[s, h],
-                p.dev(zh=zh, x=x, co=co, y=p.y - p.yl + yl),
-            )
-
-        return 0
-
-    lax.fori_loop(0, 64, take, 0)
-
-    def finish(g, _):
-        rows = [m["rx"][pl.ds(4 * g, 4), h].reshape(128, C) for h in range(HEADS)]
-        update = dot(jnp.concatenate(rows, axis=1), m["wide"][...])
-        for s in range(4):
-            for b in range(3):
-                at = pl.ds(3 * (4 * g + s) + b, 24, stride=48)
-                dst[at, :] = src[at, :] + update[32 * s : 32 * s + 24, b * 128 : b * 128 + 128]
-        return 0
-
-    lax.fori_loop(0, 4, finish, 0)
-
-    def leave(t, _):
-        z, yl, n = t // 32, (t // 16) % 2, t % 16
-        zh, x, co = 2 * z + n // 8, (n // 2) % 4, n % 2
-        y = p.y - p.yl + yl
-
-        @pl.when(
-            jnp.logical_not((zh == p.zh) & (x == p.x) & (co == p.co) & (yl == p.yl))
-        )
-        def _():
-            sent(m["rs"].at[z, yl, n], m["rt_s"].at[z, yl, n], p.dev(zh=zh, x=x, co=co, y=y))
+            sent(m["rs"].at[z, yl, n], m["rt_s"].at[z, yl, n], p.dev(zh=zh, x=x, y=y))
 
         return 0
 
     def close():
         for copy in copies:
             copy.wait_send()
-        lax.fori_loop(0, 64, leave, 0)
+        lax.fori_loop(0, 32, leave, 0)
 
     return close
 
@@ -719,7 +712,8 @@
     def ready():
         pl.semaphore_wait(barrier, len(others))
 
-    close1 = phase1(p, ready, pair, mask, proj1, bias1_w, out1_w, mid, m1)
+    nrm, nf = m2["nrm"], m2["nf"]
+    close1 = phase1(p, ready, pair, mask, proj1, bias1_w, out1_w, mid, nrm, nf, m1)
     close2 = phase2(p, mid, mask, proj2, bias2_w, out2_w, dst, m2)
     close1()
     close2()
@@ -741,12 +735,12 @@
         name="triangle_attention",
     )(
         pair.reshape(rows * cols, C),
-        residue_mask.reshape(1, -1),
+        residue_mask,
         start_proj,
-        start_bias_w,
+        start_bias_w.T,
         start_out,
         end_proj,
-        end_bias_w,
+        end_bias_w.T,
         end_out,
     )
     return out.reshape(rows, cols, C)

time: 125 us -> 109 us (0.87)
  the two profiles are of different devices: /device:TPU:127 before, /device:TPU:79 now
where the time goes in v3:
time: 109 us; the launch traced here: 108 us
  Pallas kernels  107 us (98%)
  local copies, waits for them, and re-layouts  1.92 us (2%)
    pallas_call x1, Pallas kernels, shards(): pl.pallas_call(functools.partial(kernel, tuple(one), tuple(two)), out_sha...  107 us

profile of v3, /device:TPU:79, one launch (start us, length us, event | category | flops | bytes accessed | tf_op | source)
XLA Modules:
  0.0 108.5 jit_solution(11872400625508820455)
XLA Ops:
  0.0 106.5 %triangle_attention.1 = f32[1152,128]{1,0:T(8,128)} custom-call(f32[1152,128]{1,0:T(8,128)} %bitcast.5, s32[768]{0:T(1024)} %mask.1, bf16[128,512]{1,0:T(8,128)(2,1)} %proj1.1, bf16[4,128]{1,0:T(4,128)(2,1)} %bitcast.6, bf16[128,128]{1,0:T(8,128)(2,1)} %out1_w.1, bf16[128,512]{1,0:T(8,128)(2,1)} %proj2.1, bf16[4,128]{1,0:T(4,128)(2,1)} %bitcast.7, ...), custom_call_target="tpu_custom_call" | custom-call | tf_op jit(solution)/shard_map/triangle_attention/pallas_call | solution.py:726
  106.5 1.9 %copy.10 = f32[24,48,128]{2,1,0:T(8,128)} copy(f32[24,48,128]{2,1,0:T(8,128)} %bitcast.4) | data formatting | bytes 1179648

commit v4 on v3

--- a/solution.py
+++ b/solution.py
@@ -128,6 +128,7 @@
 
 NEAR = (0, 1, 3, 2)
 FAR = (4, 3, 5, 2, 6, 1, 7, 0)
+CLOSE = FAR[::-1]
 
 
 def scratch1():
@@ -153,8 +154,8 @@
         "xy_r": dma((8,)),
         "xz_s": dma((8,)),
         "xz_r": dma((8,)),
-        "xc_s": dma((2,)),
-        "xc_r": dma((2,)),
+        "xc_s": dma((2, 8)),
+        "xc_r": dma((2, 8)),
         "bz_s": dma((4,)),
         "bz_r": dma((4,)),
         "bx_s": dma((4, 4)),
@@ -166,21 +167,14 @@
 
 def partners(p):
     out = []
-    for c in range(2):
-        for z in range(2):
-            for e in range(8):
+    for e in FAR:
+        for c in range(2):
+            for z in range(2):
                 if (c, z, e) != (0, 0, 0):
                     out.append(p.dev(co=(p.co + c) % 2, zl=(p.zl + z) % 2, y=(p.y + e) % 8))
-    for a in range(4):
-        for b in range(4):
-            if (a, b) == (0, 0):
-                continue
-            zh, x = (p.zh + a) % 4, (p.x + b) % 4
-            for co in range(2):
-                out.append(p.dev(zh=zh, x=x, co=co))
-                out.append(p.dev(zh=zh, x=x, co=co, y=p.y1))
-    for a in range(1, 4):
-        out.append(p.dev(zh=(p.zh + a) % 4, zl=1 - p.zl))
+    for d in range(1, 4):
+        out.append(p.dev(zh=(p.zh + d) % 4))
+        out.append(p.dev(x=(p.x + d) % 4))
     return out
 
 
@@ -268,7 +262,7 @@
             send(mine, mine, m["bz_s"].at[d], m["bz_r"].at[p.zh], p.dev(zh=(p.zh + d) % 4))
         )
     to_columns(p.zh)
-    for d in range(8):
+    for d in CLOSE:
         fr = (p.y + d) % 8
         block = m["x1f"].at[p.co, p.zl, fr]
         if d:
@@ -276,23 +270,22 @@
         copies.append(
             send(block, block, m["xz_s"].at[d], m["xz_r"].at[fr], p.dev(zl=(p.zl + 1) % 2))
         )
-    half = m["x1f"].at[p.co, p.zl]
-    copies.append(
-        send(half, half, m["xc_s"].at[0], m["xc_r"].at[p.zl], p.dev(co=(p.co + 1) % 2))
-    )
+        copies.append(
+            send(block, block, m["xc_s"].at[0, d], m["xc_r"].at[p.zl, fr], p.dev(co=1 - p.co))
+        )
 
     for d in NEAR[1:]:
         zh = (p.zh + d) % 4
         got(m["bf"].at[p.x, zh], m["bz_r"].at[zh], p.dev(zh=zh))
         to_columns(zh)
     other = (p.zl + 1) % 2
-    for d in range(8):
+    for d in CLOSE:
         fr = (p.y + d) % 8
-        got(m["x1f"].at[p.co, other, fr], m["xz_r"].at[fr], p.dev(zl=other))
-    half = m["x1f"].at[p.co, other]
-    copies.append(
-        send(half, half, m["xc_s"].at[1], m["xc_r"].at[other], p.dev(co=(p.co + 1) % 2))
-    )
+        block = m["x1f"].at[p.co, other, fr]
+        got(block, m["xz_r"].at[fr], p.dev(zl=other))
+        copies.append(
+            send(block, block, m["xc_s"].at[1, d], m["xc_r"].at[other, fr], p.dev(co=1 - p.co))
+        )
 
     lane = iota((768, C), 1)
 
@@ -302,7 +295,8 @@
         @pl.when(t == 1)
         def _():
             for zl in range(2):
-                got(m["x1f"].at[co, zl], m["xc_r"].at[zl], p.dev(co=co))
+                for y in range(8):
+                    got(m["x1f"].at[co, zl, y], m["xc_r"].at[zl, y], p.dev(co=co))
 
         gate = jnp.zeros((768, C), F32)
         for a in range(3):
@@ -367,7 +361,8 @@
 
     lax.fori_loop(0, 8, attend, 0)
 
-    def finish(y, _):
+    def finish(t, _):
+        y = (p.y + (1 - 2 * (t % 2)) * (t // 2) - t % 2 + 8) % 8
         for h in range(HEADS):
 
             @pl.when(jnp.logical_not((y == p.y) & (h == head)))
@@ -434,8 +429,8 @@
         "xa_r": dma((4, 4)),
         "xy_s": dma((4, 4)),
         "xy_r": dma((4, 4)),
-        "xc_s": dma((2,)),
-        "xc_r": dma((2,)),
+        "xc_s": dma((2, 4)),
+        "xc_r": dma((2, 4)),
         "bz_s": dma((4, 2)),
         "bz_r": dma((4, 2)),
         "bx_s": dma((4, 4, 2)),
@@ -453,7 +448,7 @@
     return jnp.where(hit, 1.0, 0.0).astype(BF16)
 
 
-def phase2(p, src, mask, proj, bias_w, out_w, dst, m):
+def phase2(p, mask, proj, bias_w, out_w, dst, m):
     head = 2 * p.yl + p.co
     other = 1 - p.co
     copies = []
@@ -553,8 +548,10 @@
             copies.append(
                 send(block, block, m["xy_s"].at[a, b], m["xy_r"].at[zh, x], p.dev(y=p.y1))
             )
-    part = m["x2"].at[p.yl, p.co]
-    copies.append(send(part, part, m["xc_s"].at[0], m["xc_r"].at[p.yl], p.dev(co=other)))
+        part = m["x2"].at[p.yl, p.co, zh]
+        copies.append(
+            send(part, part, m["xc_s"].at[0, a], m["xc_r"].at[p.yl, zh], p.dev(co=other))
+        )
 
     for z in range(2):
         for a in NEAR:
@@ -567,15 +564,18 @@
         for b in NEAR:
             zh, x = (p.zh + a) % 4, (p.x + b) % 4
             got(m["x2"].at[1 - p.yl, p.co, zh, x], m["xy_r"].at[zh, x], p.dev(y=p.y1))
-    part = m["x2"].at[1 - p.yl, p.co]
-    copies.append(send(part, part, m["xc_s"].at[1], m["xc_r"].at[1 - p.yl], p.dev(co=other)))
+        part = m["x2"].at[1 - p.yl, p.co, zh]
+        copies.append(
+            send(part, part, m["xc_s"].at[1, a], m["xc_r"].at[1 - p.yl, zh], p.dev(co=other))
+        )
 
     sub = iota((16, 768), 0)
     ones = jnp.where(sub == 0, 1.0, 0.0)
 
     def prepare(t, _):
         yl = (p.yl + t) % 2
-        got(m["x2"].at[yl, other], m["xc_r"].at[yl], p.dev(co=other))
+        for zh in range(4):
+            got(m["x2"].at[yl, other, zh], m["xc_r"].at[yl, zh], p.dev(co=other))
 
         def arrange(n, _):
             zh, x = n // 4, n % 4
@@ -674,7 +674,7 @@
             for b in range(3):
                 chip = update[48 * x : 48 * x + 48, b * 128 : b * 128 + 128]
                 at = pl.ds(3 * (4 * zh + x) + b, 24, stride=48)
-                dst[at, :] = src[at, :] + jnp.where(p.co == 0, chip[0:24], chip[24:48])
+                dst[at, :] = jnp.where(p.co == 0, chip[0:24], chip[24:48])
         return 0
 
     lax.fori_loop(0, 4, finish, 0)
@@ -699,7 +699,7 @@
 
 
 def kernel(
-    names1, names2, pair, mask, proj1, bias1_w, out1_w, proj2, bias2_w, out2_w, dst, mid, *refs
+    names1, names2, pair, mask, proj1, bias1_w, out1_w, proj2, bias2_w, out2_w, dst, mid_out, mid, mid_sem, *refs
 ):
     m1 = dict(zip(names1, refs))
     m2 = dict(zip(names2, refs[len(names1) :]))
@@ -714,21 +714,24 @@
 
     nrm, nf = m2["nrm"], m2["nf"]
     close1 = phase1(p, ready, pair, mask, proj1, bias1_w, out1_w, mid, nrm, nf, m1)
-    close2 = phase2(p, mid, mask, proj2, bias2_w, out2_w, dst, m2)
+    keep = pltpu.make_async_copy(mid, mid_out, mid_sem)
+    keep.start()
+    close2 = phase2(p, mask, proj2, bias2_w, out2_w, dst, m2)
     close1()
     close2()
+    keep.wait()
 
 
 def shards(pair, residue_mask, start_proj, start_bias_w, start_out, end_proj, end_bias_w, end_out):
     rows, cols = pair.shape[:2]
     one, two = scratch1(), scratch2()
     vmem = pl.BlockSpec(memory_space=pltpu.VMEM)
-    out = pl.pallas_call(
+    update, mid = pl.pallas_call(
         functools.partial(kernel, tuple(one), tuple(two)),
-        out_shape=jax.ShapeDtypeStruct((rows * cols, C), F32),
+        out_shape=[jax.ShapeDtypeStruct((rows * cols, C), F32)] * 2,
         in_specs=[vmem] * 8,
-        out_specs=vmem,
-        scratch_shapes=[pltpu.VMEM((rows * cols, C), F32)] + list(one.values()) + list(two.values()),
+        out_specs=[vmem, pl.BlockSpec(memory_space=pl.ANY)],
+        scratch_shapes=[pltpu.VMEM((rows * cols, C), F32), pltpu.SemaphoreType.DMA] + list(one.values()) + list(two.values()),
         compiler_params=pltpu.CompilerParams(
             collective_id=0, has_side_effects=True, vmem_limit_bytes=56 << 20
         ),
@@ -743,7 +746,7 @@
         end_bias_w.T,
         end_out,
     )
-    return out.reshape(rows, cols, C)
+    return (mid + update).reshape(rows, cols, C)
 
 
 def solution(mesh):

time: 109 us -> 107 us (0.982)
  the two profiles are of different devices: /device:TPU:79 before, /device:TPU:73 now
where the time goes in v4:
time: 107 us
  Pallas kernels  105 us (98%)
  other arithmetic  2.12 us (2%)
    pallas_call x1, Pallas kernels, shards(): pl.pallas_call(functools.partial(kernel, tuple(one), tuple(two)), out_sha...  105 us

profile of v4, /device:TPU:73, one launch (start us, length us, event | category | flops | bytes accessed | tf_op | source)
XLA Modules:
  0.0 107.1 jit_solution(16723115003425064891)
XLA Ops:
  0.0 105.0 %triangle_attention.1 = (f32[1152,128]{1,0:T(8,128)}, f32[1152,128]{1,0:T(8,128)}) custom-call(f32[1152,128]{1,0:T(8,128)} %bitcast.4, s32[768]{0:T(1024)} %mask.1, bf16[128,512]{1,0:T(8,128)(2,1)} %proj1.1, bf16[4,128]{1,0:T(4,128)(2,1)} %bitcast.5, bf16[128,128]{1,0:T(8,128)(2,1)} %out1_w.1, bf16[128,512]{1,0:T(8,128)(2,1)} %proj2.1, ...), custom_call_target="tpu_custom_call" | custom-call | tf_op jit(solution)/shard_map/triangle_attention/pallas_call | solution.py:729
  105.0 2.1 %add.3 = f32[1152,128]{1,0:T(8,128)} add(f32[1152,128]{1,0:T(8,128)} %get-tuple-element.7, f32[1152,128]{1,0:T(8,128)} %get-tuple-element.8) | non-fusion elementwise | flops 147456 | bytes 1769472 | tf_op jit(solution)/shard_map/add | solution.py:749

commit v5 on v4

--- a/solution.py
+++ b/solution.py
@@ -178,16 +178,14 @@
     return out
 
 
-def phase1(p, ready, src, mask, proj, bias_w, out_w, dst, nrm, nf, m):
+def phase1(p, fetches, ready, src, mask, proj, bias_w, out_w, dst, nrm, nf, m):
     head = 2 * p.zl + p.co
     copies = []
 
-    def norm_block(b, _):
-        at = pl.multiple_of(b * 144, 16)
-        m["nrm"][b] = layer_norm(src[pl.ds(at, 144), :]).astype(BF16)
-        return 0
-
-    lax.fori_loop(0, 8, norm_block, 0)
+    for b, fetch in enumerate(fetches):
+        fetch.wait()
+        normed = layer_norm(src[288 * b : 288 * b + 288, :]).astype(BF16)
+        m["nrm"][2 * b : 2 * b + 2] = normed.reshape(2, 144, C)
     local_bias(m["nrm"][...].reshape(1152, C), bias_w[...], m["spread"], m["hs"])
     ready()
     m["by"][p.co, p.zl, p.y] = m["hs"][head]
@@ -362,25 +360,27 @@
     lax.fori_loop(0, 8, attend, 0)
 
     def finish(t, _):
-        y = (p.y + (1 - 2 * (t % 2)) * (t // 2) - t % 2 + 8) % 8
-        for h in range(HEADS):
-
-            @pl.when(jnp.logical_not((y == p.y) & (h == head)))
-            def _():
-                got(m["rx"].at[y, h], m["rt_r"].at[y, h], p.dev(co=h % 2, zl=h // 2, y=y))
-
-        rows = jnp.concatenate([m["rx"][y, h] for h in range(HEADS)], axis=1)
-        update = dot(rows, m["wide"][...])
-        for a in range(3):
-            at = pl.multiple_of((3 * y + a) * 48, 16)
-            mid = src[pl.ds(at, 48), :] + update[:, a * 128 : a * 128 + 128]
-            dst[pl.ds(at, 48), :] = mid
-            normed = layer_norm(mid).astype(BF16)
-            nrm[pl.ds(at, 48), :] = normed
-            nf[pl.ds(at, 48), :] = normed.astype(F32)
+        places = [(p.y + 8 - t) % 8, (p.y + t + 1) % 8]
+        for y in places:
+            for h in range(HEADS):
+
+                @pl.when(jnp.logical_not((y == p.y) & (h == head)))
+                def _():
+                    got(m["rx"].at[y, h], m["rt_r"].at[y, h], p.dev(co=h % 2, zl=h // 2, y=y))
+
+        for y in places:
+            rows = jnp.concatenate([m["rx"][y, h] for h in range(HEADS)], axis=1)
+            update = dot(rows, m["wide"][...])
+            for a in range(3):
+                at = pl.multiple_of((3 * y + a) * 48, 16)
+                mid = src[pl.ds(at, 48), :] + update[:, a * 128 : a * 128 + 128]
+                dst[pl.ds(at, 48), :] = mid
+                normed = layer_norm(mid).astype(BF16)
+                nrm[pl.ds(at, 48), :] = normed
+                nf[pl.ds(at, 48), :] = normed.astype(F32)
         return 0
 
-    lax.fori_loop(0, 8, finish, 0)
+    lax.fori_loop(0, 4, finish, 0)
 
     def leave(t, _):
         co, zh, x = t // 16, (t // 4) % 4, t % 4
@@ -437,8 +437,8 @@
         "bx_r": dma((4, 4, 2)),
         "rt_s": dma((2, 2, 8)),
         "rt_r": dma((4, 4, 2)),
-        "rc_s": dma((4,)),
-        "rc_r": dma((4,)),
+        "rc_s": dma((4, 4)),
+        "rc_r": dma((4, 4)),
     }
 
 
@@ -448,7 +448,7 @@
     return jnp.where(hit, 1.0, 0.0).astype(BF16)
 
 
-def phase2(p, mask, proj, bias_w, out_w, dst, m):
+def phase2(p, mid, mask, proj, bias_w, out_w, dst, m):
     head = 2 * p.yl + p.co
     other = 1 - p.co
     copies = []
@@ -662,19 +662,22 @@
                         p.dev(zh=zh, x=x, y=p.y - p.yl + yl),
                     )
 
-        part = m["rx"].at[p.co, zh]
-        copies.append(send(part, part, m["rc_s"].at[d], m["rc_r"].at[zh], p.dev(co=other)))
+            part = m["rx"].at[p.co, zh, x]
+            copies.append(
+                send(part, part, m["rc_s"].at[d, x], m["rc_r"].at[zh, x], p.dev(co=other))
+            )
 
     def finish(t, _):
         zh = (p.zh + t + jnp.where(t == 2, 1, 0) - jnp.where(t == 3, 1, 0)) % 4
-        got(m["rx"].at[other, zh], m["rc_r"].at[zh], p.dev(co=other))
+        for x in range(4):
+            got(m["rx"].at[other, zh, x], m["rc_r"].at[zh, x], p.dev(co=other))
         rows = [m["rx"][h % 2, zh, :, h // 2].reshape(192, C) for h in range(HEADS)]
         update = dot(jnp.concatenate(rows, axis=1), m["wide"][...])
         for x in range(4):
             for b in range(3):
                 chip = update[48 * x : 48 * x + 48, b * 128 : b * 128 + 128]
                 at = pl.ds(3 * (4 * zh + x) + b, 24, stride=48)
-                dst[at, :] = jnp.where(p.co == 0, chip[0:24], chip[24:48])
+                dst[at, :] = mid[at, :] + jnp.where(p.co == 0, chip[0:24], chip[24:48])
         return 0
 
     lax.fori_loop(0, 4, finish, 0)
@@ -699,11 +702,16 @@
 
 
 def kernel(
-    names1, names2, pair, mask, proj1, bias1_w, out1_w, proj2, bias2_w, out2_w, dst, mid_out, mid, mid_sem, *refs
+    names1, names2, pair, mask, proj1, bias1_w, out1_w, proj2, bias2_w, out2_w, dst, mid, src, sems, *refs
 ):
     m1 = dict(zip(names1, refs))
     m2 = dict(zip(names2, refs[len(names1) :]))
     p = Place()
+    fetches = []
+    for b in range(4):
+        piece = pl.ds(288 * b, 288)
+        fetches.append(pltpu.make_async_copy(pair.at[piece], src.at[piece], sems.at[b]))
+        fetches[-1].start()
     others = partners(p)
     barrier = pltpu.get_barrier_semaphore()
     for device in others:
@@ -713,25 +721,27 @@
         pl.semaphore_wait(barrier, len(others))
 
     nrm, nf = m2["nrm"], m2["nf"]
-    close1 = phase1(p, ready, pair, mask, proj1, bias1_w, out1_w, mid, nrm, nf, m1)
-    keep = pltpu.make_async_copy(mid, mid_out, mid_sem)
-    keep.start()
-    close2 = phase2(p, mask, proj2, bias2_w, out2_w, dst, m2)
+    close1 = phase1(p, fetches, ready, src, mask, proj1, bias1_w, out1_w, mid, nrm, nf, m1)
+    close2 = phase2(p, mid, mask, proj2, bias2_w, out2_w, dst, m2)
     close1()
     close2()
-    keep.wait()
 
 
 def shards(pair, residue_mask, start_proj, start_bias_w, start_out, end_proj, end_bias_w, end_out):
     rows, cols = pair.shape[:2]
     one, two = scratch1(), scratch2()
     vmem = pl.BlockSpec(memory_space=pltpu.VMEM)
-    update, mid = pl.pallas_call(
+    out = pl.pallas_call(
         functools.partial(kernel, tuple(one), tuple(two)),
-        out_shape=[jax.ShapeDtypeStruct((rows * cols, C), F32)] * 2,
-        in_specs=[vmem] * 8,
-        out_specs=[vmem, pl.BlockSpec(memory_space=pl.ANY)],
-        scratch_shapes=[pltpu.VMEM((rows * cols, C), F32), pltpu.SemaphoreType.DMA] + list(one.values()) + list(two.values()),
+        out_shape=jax.ShapeDtypeStruct((rows * cols, C), F32),
+        in_specs=[pl.BlockSpec(memory_space=pl.ANY)] + [vmem] * 7,
+        out_specs=vmem,
+        scratch_shapes=[
+            pltpu.VMEM((rows * cols, C), F32),
+            pltpu.VMEM((rows * cols, C), F32),
+            pltpu.SemaphoreType.DMA((4,)),
+        ]
+        + list(one.values()) + list(two.values()),
         compiler_params=pltpu.CompilerParams(
             collective_id=0, has_side_effects=True, vmem_limit_bytes=56 << 20
         ),
@@ -746,7 +756,7 @@
         end_bias_w.T,
         end_out,
     )
-    return (mid + update).reshape(rows, cols, C)
+    return out.reshape(rows, cols, C)
 
 
 def solution(mesh):

time: 107 us -> 107 us (level)
  the two profiles are of different devices: /device:TPU:73 before, /device:TPU:79 now
where the time goes in v5:
time: 107 us; the launch traced here: 106 us
  Pallas kernels  104 us (97%)
  local copies, waits for them, and re-layouts  1.92 us (2%)
    pallas_call x1, Pallas kernels, shards(): pl.pallas_call(functools.partial(kernel, tuple(one), tuple(two)), out_sha...  104 us

profile of v5, /device:TPU:79, one launch (start us, length us, event | category | flops | bytes accessed | tf_op | source)
XLA Modules:
  0.0 106.4 jit_solution(17844728843018186420)
XLA Ops:
  0.0 104.4 %triangle_attention.1 = f32[1152,128]{1,0:T(8,128)} custom-call(f32[1152,128]{1,0:T(8,128)} %bitcast.5, s32[768]{0:T(1024)} %mask.1, bf16[128,512]{1,0:T(8,128)(2,1)} %proj1.1, bf16[4,128]{1,0:T(4,128)(2,1)} %bitcast.6, bf16[128,128]{1,0:T(8,128)(2,1)} %out1_w.1, bf16[128,512]{1,0:T(8,128)(2,1)} %proj2.1, bf16[4,128]{1,0:T(4,128)(2,1)} %bitcast.7, ...), custom_call_target="tpu_custom_call" | custom-call | tf_op jit(solution)/shard_map/triangle_attention/pallas_call | solution.py:734
  104.4 1.9 %copy.10 = f32[24,48,128]{2,1,0:T(8,128)} copy(f32[24,48,128]{2,1,0:T(8,128)} %bitcast.4) | data formatting | bytes 1179648

commit v6 on v5

--- a/solution.py
+++ b/solution.py
@@ -64,6 +64,11 @@
     pltpu.make_async_remote_copy(
         src_ref=src, dst_ref=src, send_sem=sem, recv_sem=sem, device_id=device, device_id_type=MESH
     ).wait_send()
+
+
+def wait_all(copies):
+    for copy in copies:
+        copy.wait()
 
 
 def layer_norm(field):
@@ -178,7 +183,7 @@
     return out
 
 
-def phase1(p, fetches, ready, src, mask, proj, bias_w, out_w, dst, nrm, nf, m):
+def phase1(p, fetches, fetched, ready, src, mask, proj, bias_w, out_w, dst, nrm, nf, m):
     head = 2 * p.zl + p.co
     copies = []
 
@@ -216,6 +221,7 @@
         )
     m["x1f"][p.co, p.zl, p.y] = m["nrm"][p.y]
 
+    fetched()
     for a in range(3):
         first, here = pick(head, 0), pick(head, 32 * a)
         m["wall"][a, :, 0:128] = dot(proj[:, 0:128], first).astype(BF16)
@@ -448,7 +454,7 @@
     return jnp.where(hit, 1.0, 0.0).astype(BF16)
 
 
-def phase2(p, mid, mask, proj, bias_w, out_w, dst, m):
+def phase2(p, close1, fetched, mid, mask, proj, bias_w, out_w, dst, m):
     head = 2 * p.yl + p.co
     other = 1 - p.co
     copies = []
@@ -489,12 +495,14 @@
                     )
                 )
 
+    fetched()
     m["wk"][...] = dot(proj[:, 128:256], pick(head, 0)).astype(BF16)
     wt = dot_nt(pick_rows(head, 0), proj[:, 0:128])
     wt = wt + dot_nt(pick_rows(head, 32), proj[:, 256:384])
     wt = wt + dot_nt(pick_rows(head, 64), proj[:, 384:512])
     m["wt"][...] = wt.astype(BF16)
     spread_out(out_w, m["wide"])
+    close1()
 
     row, col = iota((48, 768), 0), iota((48, 768), 1)
     keep = jnp.where(col == row + 48 * (4 * p.zh + p.x), mask[...].reshape(1, 768), 0)
@@ -649,6 +657,10 @@
 
     lax.fori_loop(0, 4, attend, 0)
 
+    for copy in copies:
+        copy.wait_send()
+    copies.clear()
+
     for d in NEAR:
         zh = (p.zh + d) % 4
         for x in range(4):
@@ -702,7 +714,7 @@
 
 
 def kernel(
-    names1, names2, pair, mask, proj1, bias1_w, out1_w, proj2, bias2_w, out2_w, dst, mid, src, sems, *refs
+    names1, names2, pair, mask, proj1, bias1_w, out1_w, proj2, bias2_w, out2_w, dst, mid, src, proj1_v, out1_v, proj2_v, out2_v, sems, *refs
 ):
     m1 = dict(zip(names1, refs))
     m2 = dict(zip(names2, refs[len(names1) :]))
@@ -712,6 +724,12 @@
         piece = pl.ds(288 * b, 288)
         fetches.append(pltpu.make_async_copy(pair.at[piece], src.at[piece], sems.at[b]))
         fetches[-1].start()
+    weights = []
+    for n, (given, held) in enumerate(
+        zip((proj1, out1_w, proj2, out2_w), (proj1_v, out1_v, proj2_v, out2_v))
+    ):
+        weights.append(pltpu.make_async_copy(given, held, sems.at[4 + n]))
+        weights[-1].start()
     others = partners(p)
     barrier = pltpu.get_barrier_semaphore()
     for device in others:
@@ -721,25 +739,30 @@
         pl.semaphore_wait(barrier, len(others))
 
     nrm, nf = m2["nrm"], m2["nf"]
-    close1 = phase1(p, fetches, ready, src, mask, proj1, bias1_w, out1_w, mid, nrm, nf, m1)
-    close2 = phase2(p, mid, mask, proj2, bias2_w, out2_w, dst, m2)
-    close1()
+    fetched1 = functools.partial(wait_all, weights[:2])
+    fetched2 = functools.partial(wait_all, weights[2:])
+    close1 = phase1(p, fetches, fetched1, ready, src, mask, proj1_v, bias1_w, out1_v, mid, nrm, nf, m1)
+    close2 = phase2(p, close1, fetched2, mid, mask, proj2_v, bias2_w, out2_v, dst, m2)
     close2()
 
 
 def shards(pair, residue_mask, start_proj, start_bias_w, start_out, end_proj, end_bias_w, end_out):
     rows, cols = pair.shape[:2]
     one, two = scratch1(), scratch2()
-    vmem = pl.BlockSpec(memory_space=pltpu.VMEM)
+    vmem, hbm = pl.BlockSpec(memory_space=pltpu.VMEM), pl.BlockSpec(memory_space=pl.ANY)
     out = pl.pallas_call(
         functools.partial(kernel, tuple(one), tuple(two)),
         out_shape=jax.ShapeDtypeStruct((rows * cols, C), F32),
-        in_specs=[pl.BlockSpec(memory_space=pl.ANY)] + [vmem] * 7,
+        in_specs=[hbm, vmem, hbm, vmem, hbm, hbm, vmem, hbm],
         out_specs=vmem,
         scratch_shapes=[
             pltpu.VMEM((rows * cols, C), F32),
             pltpu.VMEM((rows * cols, C), F32),
-            pltpu.SemaphoreType.DMA((4,)),
+            pltpu.VMEM(start_proj.shape, BF16),
+            pltpu.VMEM(start_out.shape, BF16),
+            pltpu.VMEM(end_proj.shape, BF16),
+            pltpu.VMEM(end_out.shape, BF16),
+            pltpu.SemaphoreType.DMA((8,)),
         ]
         + list(one.values()) + list(two.values()),
         compiler_params=pltpu.CompilerParams(

time: 107 us -> 106 us (level)
  no operation moved by 1% of the time
where the time goes in v6:
time: 106 us; the launch traced here: 105 us
  Pallas kernels  103 us (97%)
  local copies, waits for them, and re-layouts  1.92 us (2%)
    pallas_call x1, Pallas kernels, shards(): pl.pallas_call(functools.partial(kernel, tuple(one), tuple(two)), out_sha...  103 us

profile of v6, /device:TPU:79, one launch (start us, length us, event | category | flops | bytes accessed | tf_op | source)
XLA Modules:
  0.0 105.3 jit_solution(9825684951287409704)
XLA Ops:
  0.0 103.4 %triangle_attention.1 = f32[1152,128]{1,0:T(8,128)} custom-call(f32[1152,128]{1,0:T(8,128)} %bitcast.5, s32[768]{0:T(1024)} %mask.1, bf16[128,512]{1,0:T(8,128)(2,1)} %proj1.1, bf16[4,128]{1,0:T(4,128)(2,1)} %bitcast.6, bf16[128,128]{1,0:T(8,128)(2,1)} %out1_w.1, bf16[128,512]{1,0:T(8,128)(2,1)} %proj2.1, bf16[4,128]{1,0:T(4,128)(2,1)} %bitcast.7, ...), custom_call_target="tpu_custom_call" | custom-call | tf_op jit(solution)/shard_map/triangle_attention/pallas_call | solution.py:753
  103.4 1.9 %copy.10 = f32[24,48,128]{2,1,0:T(8,128)} copy(f32[24,48,128]{2,1,0:T(8,128)} %bitcast.4) | data formatting | bytes 1179648

commit v7 on v6

--- a/solution.py
+++ b/solution.py
@@ -221,6 +221,16 @@
         )
     m["x1f"][p.co, p.zl, p.y] = m["nrm"][p.y]
 
+    def hand_on(d):
+        fr = (p.y + d) % 8
+        block = m["x1f"].at[p.co, p.zl, fr]
+        copies.append(send(block, block, m["xz_s"].at[d], m["xz_r"].at[fr], p.dev(zl=1 - p.zl)))
+        copies.append(
+            send(block, block, m["xc_s"].at[0, d], m["xc_r"].at[p.zl, fr], p.dev(co=1 - p.co))
+        )
+
+    hand_on(0)
+
     fetched()
     for a in range(3):
         first, here = pick(head, 0), pick(head, 32 * a)
@@ -266,17 +276,10 @@
             send(mine, mine, m["bz_s"].at[d], m["bz_r"].at[p.zh], p.dev(zh=(p.zh + d) % 4))
         )
     to_columns(p.zh)
-    for d in CLOSE:
+    for d in CLOSE[1:]:
         fr = (p.y + d) % 8
-        block = m["x1f"].at[p.co, p.zl, fr]
-        if d:
-            got(block, m["xy_r"].at[fr], p.dev(y=fr))
-        copies.append(
-            send(block, block, m["xz_s"].at[d], m["xz_r"].at[fr], p.dev(zl=(p.zl + 1) % 2))
-        )
-        copies.append(
-            send(block, block, m["xc_s"].at[0, d], m["xc_r"].at[p.zl, fr], p.dev(co=1 - p.co))
-        )
+        got(m["x1f"].at[p.co, p.zl, fr], m["xy_r"].at[fr], p.dev(y=fr))
+        hand_on(d)
 
     for d in NEAR[1:]:
         zh = (p.zh + d) % 4
@@ -484,6 +487,10 @@
             m["ns"][zh, x] = jnp.concatenate(rows, axis=0).astype(BF16)
             if (a, b) == (0, 0):
                 m["x2"][p.yl, p.co, p.zh, p.x] = m["ns"][zh, x]
+                block = m["x2"].at[p.yl, p.co, p.zh, p.x]
+                copies.append(
+                    send(block, block, m["xy_s"].at[0, 0], m["xy_r"].at[zh, x], p.dev(y=p.y1))
+                )
             else:
                 copies.append(
                     send(
@@ -553,9 +560,9 @@
             block = m["x2"].at[p.yl, p.co, zh, x]
             if (a, b) != (0, 0):
                 got(block, m["xa_r"].at[zh, x], p.dev(zh=zh, x=x))
-            copies.append(
-                send(block, block, m["xy_s"].at[a, b], m["xy_r"].at[zh, x], p.dev(y=p.y1))
-            )
+                copies.append(
+                    send(block, block, m["xy_s"].at[a, b], m["xy_r"].at[zh, x], p.dev(y=p.y1))
+                )
         part = m["x2"].at[p.yl, p.co, zh]
         copies.append(
             send(part, part, m["xc_s"].at[0, a], m["xc_r"].at[p.yl, zh], p.dev(co=other))

time: 106 us -> 105 us (level)
  no operation moved by 1% of the time
where the time goes in v7:
time: 105 us
  Pallas kernels  103 us (98%)
  local copies, waits for them, and re-layouts  1.92 us (2%)
    pallas_call x1, Pallas kernels, shards(): pl.pallas_call(functools.partial(kernel, tuple(one), tuple(two)), out_sha...  103 us

profile of v7, /device:TPU:79, one launch (start us, length us, event | category | flops | bytes accessed | tf_op | source)
XLA Modules:
  0.0 104.7 jit_solution(1975321641916660163)
XLA Ops:
  0.0 102.8 %triangle_attention.1 = f32[1152,128]{1,0:T(8,128)} custom-call(f32[1152,128]{1,0:T(8,128)} %bitcast.5, s32[768]{0:T(1024)} %mask.1, bf16[128,512]{1,0:T(8,128)(2,1)} %proj1.1, bf16[4,128]{1,0:T(4,128)(2,1)} %bitcast.6, bf16[128,128]{1,0:T(8,128)(2,1)} %out1_w.1, bf16[128,512]{1,0:T(8,128)(2,1)} %proj2.1, bf16[4,128]{1,0:T(4,128)(2,1)} %bitcast.7, ...), custom_call_target="tpu_custom_call" | custom-call | tf_op jit(solution)/shard_map/triangle_attention/pallas_call | solution.py:760
  102.8 1.9 %copy.10 = f32[24,48,128]{2,1,0:T(8,128)} copy(f32[24,48,128]{2,1,0:T(8,128)} %bitcast.4) | data formatting | bytes 1179648
